TPU v7x, 256 devices: a whole 4x4x8 slice. The times are simulated.
256 devices in a mesh: dp: 64 (over z, y, core), tensor: 4 (over x).
Axes of the slice: x: 4, y: 4, z: 8, core: 2. Of those that a mesh axis runs over, the one named last changes fastest.
Arguments:
- query: bfloat16 [512, 8192], P('dp', 'tensor'), may hold values from -8 to 8
- incoming_key: bfloat16 [512, 1024], P('dp', 'tensor'), may hold values from -5 to 5
- incoming_value: bfloat16 [512, 1024], P('dp', 'tensor'), may hold values from -5 to 5
- cycle_key_cache: bfloat16 [512, 1024, 1024], P('dp', None, 'tensor'), may hold values from -8 to 8
- cycle_value_cache: bfloat16 [512, 1024, 1024], P('dp', None, 'tensor'), may hold values from -5 to 5
- position: int32 [512], P('dp'), may hold values from 1 to 2047
- tenant: int32 [512], replicated, may hold values from 0 to 511
- tenant_adapter_index: int32 [512], replicated, may hold values from 0 to 511, each once
- output_weight: bfloat16 [8192, 8192], P('tensor', 'dp'), may hold values from -0.5 to 0.5
- adapter_down_weight: bfloat16 [512, 8192, 64], P('dp', 'tensor'), may hold values from -0.5 to 0.5
- adapter_up_weight: bfloat16 [512, 64, 8192], P('dp', None, 'tensor'), may hold values from -0.75 to 0.75
Outputs:
- mixed: bfloat16 [512, 8192], P('dp', 'tensor')
All inputs are finite; a program needn't handle non-finite values.
Results may differ from a plain program's by a relative error of at most 0.012.
Values may be sent and summed in bfloat16 or wider, within the bound.
No kernel may reach another device: no remote copies, remote signals or barrier semaphores. Data moves between devices by JAX's collectives and lax.ppermute only.
A program may use at most 64 MiB of HBM per device.

v0:
```python
import jax
import jax.numpy as jnp
from jax import lax
from jax.sharding import PartitionSpec as P

HEAD_SIZE = 128


adapter_scale = 0.5


def attend(query, incoming_key, incoming_value, cycle_key_cache, cycle_value_cache, position):
    sessions = query.shape[0]
    cache_len = cycle_key_cache.shape[1]
    heads_kv = cycle_key_cache.shape[2] // HEAD_SIZE
    group = query.shape[1] // (heads_kv * HEAD_SIZE)
    inverse = HEAD_SIZE ** (-0.5)
    slots = jnp.arange(cache_len, dtype=jnp.int32)
    here = slots[None, :] == (position % cache_len)[:, None]
    live = (slots[None, :] < position[:, None]) & jnp.logical_not(here)
    query4 = query.reshape(sessions, heads_kv, group, HEAD_SIZE)
    keys4 = cycle_key_cache.reshape(sessions, cache_len, heads_kv, HEAD_SIZE)
    values4 = cycle_value_cache.reshape(sessions, cache_len, heads_kv, HEAD_SIZE)
    scores = (
        jnp.einsum("skgd,sckd->skgc", query4, keys4, preferred_element_type=jnp.float32) * inverse
    )
    fresh = (
        jnp.einsum(
            "skgd,skd->skg",
            query4,
            incoming_key.reshape(sessions, heads_kv, HEAD_SIZE),
            preferred_element_type=jnp.float32,
        )
        * inverse
    )
    scores = jnp.where(live[:, None, None, :], scores, jnp.float32(-1e30))
    top = jnp.maximum(jnp.max(scores, axis=-1), fresh)
    weights = jnp.exp(scores - top[..., None])
    fresh_weight = jnp.exp(fresh - top)
    total = jnp.sum(weights, axis=-1) + fresh_weight
    probs = (weights / total[..., None]).astype(jnp.bfloat16)
    fresh_prob = (fresh_weight / total).astype(jnp.bfloat16)
    attended = jnp.einsum("skgc,sckd->skgd", probs, values4, preferred_element_type=jnp.float32)
    attended = attended + fresh_prob.astype(jnp.float32)[..., None] * incoming_value.reshape(
        sessions, heads_kv, 1, HEAD_SIZE
    ).astype(jnp.float32)
    return attended.reshape(sessions, heads_kv * group * HEAD_SIZE).astype(jnp.bfloat16)


def local(
    query,
    incoming_key,
    incoming_value,
    cycle_key_cache,
    cycle_value_cache,
    position,
    tenant,
    tenant_adapter_index,
    output_weight,
    adapter_down_weight,
    adapter_up_weight,
):
    kept_state = adapter_down_weight.shape[0]
    rank_extent = adapter_down_weight.shape[2]
    block_cols = output_weight.shape[1]
    fourth_portion = adapter_up_weight.shape[2]
    attended = attend(
        query, incoming_key, incoming_value, cycle_key_cache, cycle_value_cache, position
    )
    partial_result = lax.all_gather(attended, "dp", axis=0, tiled=True)
    rows = partial_result.shape[0]
    base_part = jnp.dot(partial_result, output_weight, preferred_element_type=jnp.float32)
    rank_portion = jnp.einsum(
        "mj,hju->mhu", partial_result, adapter_down_weight, preferred_element_type=jnp.float32
    )
    projected = jnp.concatenate(
        [base_part, rank_portion.reshape(rows, kept_state * rank_extent)], axis=1
    )
    everyone = projected.shape[0]
    base_part = projected[:, :block_cols]
    rank_portion = projected[:, block_cols:].reshape(everyone, kept_state, rank_extent)
    home = lax.axis_index("dp")
    tenants_all = tenant_adapter_index.shape[0]
    matches = tenant[:, None] == jnp.arange(tenants_all, dtype=jnp.int32)[None, :]
    slot_of = jnp.sum(jnp.where(matches, tenant_adapter_index[None, :], 0), axis=1)
    my_slots = home * kept_state + jnp.arange(kept_state, dtype=jnp.int32)
    mine = slot_of[:, None] == my_slots[None, :]
    rank_local = jnp.sum(jnp.where(mine[:, :, None], rank_portion, 0.0), axis=1)
    rank_full = lax.psum(rank_local, "tensor")
    rank_spread = jnp.where(mine[:, :, None], rank_full[:, None, :], 0.0).astype(jnp.bfloat16)
    rank_spread = rank_spread.reshape(everyone, kept_state * rank_extent)
    adapter_delta = jnp.dot(
        rank_spread,
        adapter_up_weight.reshape(kept_state * rank_extent, fourth_portion),
        preferred_element_type=jnp.float32,
    ).astype(jnp.bfloat16)
    routed = lax.all_to_all(base_part, "dp", split_axis=0, concat_axis=1, tiled=True)
    base_output_sum = lax.psum_scatter(routed, "tensor", scatter_dimension=1, tiled=True)
    adapter_delta_sum = lax.psum_scatter(
        adapter_delta.astype(jnp.float32), "dp", scatter_dimension=0, tiled=True
    )
    return (base_output_sum + adapter_scale * adapter_delta_sum).astype(jnp.bfloat16)


def solution(mesh):
    return jax.shard_map(
        local,
        mesh=mesh,
        in_specs=(
            P("dp", "tensor"),
            P("dp", "tensor"),
            P("dp", "tensor"),
            P("dp", None, "tensor"),
            P("dp", None, "tensor"),
            P("dp"),
            P(),
            P(),
            P("tensor", "dp"),
            P("dp", "tensor", None),
            P("dp", None, "tensor"),
        ),
        out_specs=P("dp", "tensor"),
        check_vma=False,
    )
```

profile of v0, /device:TPU:6, one launch (start us, length us, event | category | flops | bytes accessed | tf_op | source)
XLA Modules:
  0.0 345.0 jit_solution(14420877195557605657)
XLA Ops:
  6.5 0.0 copy-start
  6.5 0.0 copy-start.3
  6.5 0.0 all-gather.2.cloned.1.call-start
  6.5 0.0 copy-start.6
  6.5 0.8 and_select_fusion
  7.4 1.3 fusion.30
  8.7 0.9 fusion.32
  9.6 3.5 %fusion.40 = (f32[8,2,8]{2,1,0:T(2,128)S(1)}, f32[8,2,8,1024]{3,2,1,0:T(8,128)S(1)}) fusion(bf16[8,2,8,128]{3,0,2,1:T(8,128)(2,1)} %bitcast.65, pred[8,1024]{1,0:T(8,128)(4,1)S(1)} %fusion.30, bf16[8,1024,256]{2,1,0:T(8,128)(2,1)} %param.14), kind=kOutput, calls=%fused_computation.51 | convolution fusion | flops 33947520 | bytes 4760064 | tf_op jit(solution)/shard_map/skgd,sckd->skgc/dot_general | solution.py:25
  13.1 0.0 copy-start.4
  13.1 0.0 copy-start.5
  13.1 0.0 copy-start.2
  13.1 0.2 fusion.25
  13.4 0.0 copy-done.3
  13.4 0.0 copy-done.6
  13.4 0.7 fusion.19
  14.2 0.6 copy.58
  14.8 0.0 all-gather.2.cloned.1.call-update
  14.8 0.0 copy-done.4
  14.9 0.0 copy-done.5
  14.9 0.2 select_reduce_fusion.1
  15.1 0.1 broadcast_compare_fusion
  15.2 80.0 %all-gather.2.cloned.1.call-done = bf16[512,2048]{1,0:T(8,128)(2,1)} async-done(((bf16[8,2048]{1,0:T(8,128)(2,1)}), bf16[512,2048]{1,0:T(8,128)(2,1)}) %all-gather.2.cloned.1.call-update) | async-done | bytes 2097168 | tf_op jit(solution)/shard_map/all_gather | solution.py:70
  95.2 0.0 copy-done.2
  95.2 3.0 convolution_bitcast_fusion
  98.2 6.8 %all-to-all-start = ((f32[64,8,128]{2,1,0:T(8,128)}), f32[64,8,128]{2,1,0:T(8,128)S(1)}, u32[]{:S(2)}, u32[]{:S(2)}) async-start(f32[64,8,128]{2,1,0:T(8,128)} %convolution_bitcast_fusion), calls=%async_computation | async-start | bytes 524288 | tf_op jit(solution)/shard_map/all_to_all | solution.py:97
  105.1 0.0 reduce-scatter.2.cloned.1.call-start
  105.1 0.0 copy-done
  105.1 2.9 fusion.41
  108.0 0.1 select_reduce_fusion
  108.1 9.9 %all-to-all-done = f32[64,8,128]{2,1,0:T(8,128)S(1)} async-done(((f32[64,8,128]{2,1,0:T(8,128)}), f32[64,8,128]{2,1,0:T(8,128)S(1)}, u32[]{:S(2)}, u32[]{:S(2)}) %all-to-all-start) | async-done | bytes 262176 | tf_op jit(solution)/shard_map/all_to_all | solution.py:97
  118.0 0.0 copy-start.1
  118.0 0.7 copy-done.1
  118.8 0.0 reduce-scatter.2.cloned.1.call-update
  118.8 0.0 all-reduce.4.cloned.1.call-start
  118.8 15.7 %all-reduce.5 = bf16[512,64]{0,1:T(8,128)(2,1)S(1)} all-reduce(f32[512,64]{0,1:T(8,128)S(1)} %select_reduce_fusion), channel_id=1, replica_groups=mesh['dp'=64,'tensor'=4] {'tensor'}, use_global_device_ids=true, to_apply=%region_5.6 | all-reduce | flops 32768 | bytes 196608 | tf_op jit(solution)/shard_map/psum | solution.py:89
  134.6 0.0 copy-start.7
  134.6 4.9 %fusion.6 = f32[512,2048]{1,0:T(8,128)} fusion(bf16[8,64,2048]{2,1,0:T(8,128)(2,1)} %param.21, bf16[512,64]{0,1:T(8,128)(2,1)S(1)} %all-reduce.5, pred[512,8]{0,1:T(8,128)(4,1)S(1)} %broadcast_compare_fusion), kind=kOutput, calls=%fused_computation.7 | convolution fusion | flops 1076101120 | bytes 6361088 | tf_op jit(solution)/shard_map/dot_general | solution.py:92
  139.5 0.0 all-reduce.4.cloned.1.call-update
  139.5 0.0 copy-done.7
  139.5 0.6 dynamic-slice
  140.8 0.0 reduce-scatter.2.cloned.1.call-done
  140.8 196.2 %all-reduce.4.cloned.1.call-done = f32[512,2048]{1,0:T(8,128)} async-done(((f32[512,2048]{1,0:T(8,128)}), f32[512,2048]{1,0:T(8,128)}) %all-reduce.4.cloned.1.call-update) | async-done | bytes 4194320
  337.0 1.5 fusion.29
  (5 shorter events, 0.0 us)
Async XLA Ops:
  6.5 98.6 %copy-start = (bf16[8,2048,64]{1,2,0:T(8,128)(2,1)S(1)}, bf16[8,2048,64]{1,2,0:T(8,128)(2,1)}, u32[]{:S(2)}) copy-start(bf16[8,2048,64]{1,2,0:T(8,128)(2,1)} %param.20) | copy-start | bytes 6291460
  6.5 6.8 %copy-start.3 = (bf16[8,256]{1,0:T(8,128)(2,1)S(1)}, bf16[8,256]{1,0:T(8,128)(2,1)}, u32[]{:S(2)}) copy-start(bf16[8,256]{1,0:T(8,128)(2,1)} %param.13) | copy-start | bytes 12292
  6.5 88.6 %all-gather.2.cloned.1.call-start = ((), (), s32[]{:S(2)}) async-start(), calls=%async_computation.2 | async-start | bytes 2129920 | tf_op jit(solution)/shard_map/all_gather | solution.py:70
  6.5 6.9 %copy-start.6 = (bf16[8,1024,256]{2,1,0:T(8,128)(2,1)S(1)}, bf16[8,1024,256]{2,1,0:T(8,128)(2,1)}, u32[]{:S(2)}) copy-start(bf16[8,1024,256]{2,1,0:T(8,128)(2,1)} %param.15) | copy-start | bytes 12582916
  13.1 1.8 copy-start.4
  13.1 1.8 copy-start.5
  13.1 82.1 %copy-start.2 = (bf16[2048,128]{1,0:T(8,128)(2,1)S(1)}, bf16[2048,128]{1,0:T(8,128)(2,1)}, u32[]{:S(2)}) copy-start(bf16[2048,128]{1,0:T(8,128)(2,1)} %param.19) | copy-start | bytes 1572868
  98.2 19.8 %all-to-all-start = ((f32[64,8,128]{2,1,0:T(8,128)}), f32[64,8,128]{2,1,0:T(8,128)S(1)}, u32[]{:S(2)}, u32[]{:S(2)}) async-start(f32[64,8,128]{2,1,0:T(8,128)} %convolution_bitcast_fusion), calls=%async_computation | async-start | bytes 524288 | tf_op jit(solution)/shard_map/all_to_all | solution.py:97
  105.1 35.7 %reduce-scatter.2.cloned.1.call-start = ((), (), s32[]{:S(2)}) async-start(), calls=%async_computation.3 | async-start | bytes 327680 | tf_op jit(solution)/shard_map/reduce_scatter | solution.py:98
  118.0 0.7 copy-start.1
  118.8 218.2 %all-reduce.4.cloned.1.call-start = ((), (), s32[]{:S(2)}) async-start(), calls=%async_computation.4 | async-start | bytes 8388608
  134.6 4.9 %copy-start.7 = (u32[256]{0:T(256)S(1)}, u32[256]{0:T(256)}, u32[]{:S(2)}) copy-start(u32[256]{0:T(256)} %constant.45) | copy-start | bytes 3076
Sparse Core Ops, SparseCore 0:
  14.9 80.1 all-gather.1
  118.9 17.0 reduce-scatter.1
  139.9 196.9 all-reduce.3
where the time goes:
time: 345 us
  waiting for transfers between devices  286 us (83%)
  matrix products  15.9 us (5%)
  blocking collectives  15.7 us (5%)
  between operations  13.9 us (4%)
  starting transfers between devices  6.93 us (2%)
  other arithmetic  4.35 us (1%)
    unnamed x4, waiting for transfers between devices  196 us
    all_gather x1, waiting for transfers between devices, local(): partial_result = lax.all_gather(attended, 'dp', axis=0, tiled=True)  80 us
    psum x1, blocking collectives, local(): rank_full = lax.psum(rank_local, 'tensor')  15.7 us
    all_to_all x1, waiting for transfers between devices, local(): lax.all_to_all(base_part, 'dp', split_axis=0, concat_axis=1, tiled=True)  9.9 us
  transfers between devices with their start and end apart: 4, of which 3 were waited for; matrix products, arithmetic and copies ran while one was open for 3% of the time, Pallas kernels for 0%

commit v1 on v0

v1 whole, which is shorter than its diff:
```python
import jax
import jax.numpy as jnp
import numpy as np
from jax import lax
from jax.sharding import Mesh, PartitionSpec as P

HEAD_SIZE = 128
adapter_scale = 0.5
NZ, NY, NC, NX = 8, 4, 2, 4
DP = ("z", "y", "c")


def attend(query, incoming_key, incoming_value, cycle_key_cache, cycle_value_cache, position):
    sessions = query.shape[0]
    cache_len = cycle_key_cache.shape[1]
    heads_kv = cycle_key_cache.shape[2] // HEAD_SIZE
    group = query.shape[1] // (heads_kv * HEAD_SIZE)
    inverse = HEAD_SIZE ** (-0.5)
    slots = jnp.arange(cache_len, dtype=jnp.int32)
    here = slots[None, :] == (position % cache_len)[:, None]
    live = (slots[None, :] < position[:, None]) & jnp.logical_not(here)
    query4 = query.reshape(sessions, heads_kv, group, HEAD_SIZE)
    keys4 = cycle_key_cache.reshape(sessions, cache_len, heads_kv, HEAD_SIZE)
    values4 = cycle_value_cache.reshape(sessions, cache_len, heads_kv, HEAD_SIZE)
    scores = (
        jnp.einsum("skgd,sckd->skgc", query4, keys4, preferred_element_type=jnp.float32) * inverse
    )
    fresh = (
        jnp.einsum(
            "skgd,skd->skg",
            query4,
            incoming_key.reshape(sessions, heads_kv, HEAD_SIZE),
            preferred_element_type=jnp.float32,
        )
        * inverse
    )
    scores = jnp.where(live[:, None, None, :], scores, jnp.float32(-1e30))
    top = jnp.maximum(jnp.max(scores, axis=-1), fresh)
    weights = jnp.exp(scores - top[..., None])
    fresh_weight = jnp.exp(fresh - top)
    total = jnp.sum(weights, axis=-1) + fresh_weight
    probs = (weights / total[..., None]).astype(jnp.bfloat16)
    fresh_prob = (fresh_weight / total).astype(jnp.bfloat16)
    attended = jnp.einsum("skgc,sckd->skgd", probs, values4, preferred_element_type=jnp.float32)
    attended = attended + fresh_prob.astype(jnp.float32)[..., None] * incoming_value.reshape(
        sessions, heads_kv, 1, HEAD_SIZE
    ).astype(jnp.float32)
    return attended.reshape(sessions, heads_kv * group * HEAD_SIZE).astype(jnp.bfloat16)


def swap_cores(x):
    return lax.ppermute(x, "c", [(0, 1), (1, 0)])


def local(
    query,
    incoming_key,
    incoming_value,
    cycle_key_cache,
    cycle_value_cache,
    position,
    tenant,
    tenant_adapter_index,
    output_weight,
    adapter_down_weight,
    adapter_up_weight,
):
    bf16, f32 = jnp.bfloat16, jnp.float32
    kept = adapter_down_weight.shape[0]
    rank = adapter_down_weight.shape[2]
    features = adapter_down_weight.shape[1]
    cols = output_weight.shape[1]
    quarter = adapter_up_weight.shape[2]
    mine_n = query.shape[0]
    half = NY * NZ * mine_n
    core = lax.axis_index("c")
    home = lax.axis_index(DP)
    x_here = lax.axis_index("x")

    attended = attend(
        query, incoming_key, incoming_value, cycle_key_cache, cycle_value_cache, position
    )

    along_z = lax.all_to_all(
        jnp.broadcast_to(attended[None], (NZ,) + attended.shape), "z", 0, 0, tiled=True
    ).reshape(NZ * mine_n, features)
    own = lax.all_to_all(
        jnp.broadcast_to(along_z[None], (NY,) + along_z.shape), "y", 0, 0, tiled=True
    ).reshape(half, features)
    other = swap_cores(own)

    tenants_all = tenant_adapter_index.shape[0]
    matches = tenant[:, None] == jnp.arange(tenants_all, dtype=jnp.int32)[None, :]
    slot_of = jnp.sum(jnp.where(matches, tenant_adapter_index[None, :], 0), axis=1)
    slot_by_core = slot_of.reshape(NZ, NY, NC, mine_n).transpose(2, 1, 0, 3).reshape(NC, half)
    slot_own = jnp.where(core == 0, slot_by_core[0], slot_by_core[1])
    slot_other = jnp.where(core == 0, slot_by_core[1], slot_by_core[0])
    my_slots = home * kept + jnp.arange(kept, dtype=jnp.int32)

    down = adapter_down_weight

    def rank_terms(rows, slots):
        portion = jnp.einsum("mj,hju->hum", rows, down, preferred_element_type=f32)
        mine = slots[None, :] == my_slots[:, None]
        return jnp.sum(jnp.where(mine[:, None, :], portion, 0.0), axis=0)

    rank_part = jnp.concatenate(
        [rank_terms(own, slot_own), rank_terms(other, slot_other)], axis=1
    ).astype(bf16)
    base_part = jnp.concatenate(
        [
            jnp.dot(own, output_weight, preferred_element_type=f32),
            jnp.dot(other, output_weight, preferred_element_type=f32),
        ],
        axis=0,
    ).astype(bf16)

    rank_full = rank_part.astype(f32)
    for shift in (2, 1, 3):
        got = lax.ppermute(rank_part, "x", [(i, (i + shift) % NX) for i in range(NX)])
        rank_full = rank_full + got.astype(f32)
    rank_full = rank_full.astype(bf16)

    root = lax.axis_index("z") // (NZ // NX)
    base_full = base_part.astype(f32)
    for shift in (2, 1, 3):
        pairs = []
        for z in range(NZ):
            dst = z // (NZ // NX)
            src = (dst - shift) % NX
            pairs.append((z * NX + src, z * NX + dst))
        got = lax.ppermute(base_part, ("z", "x"), pairs)
        base_full = base_full + got.astype(f32)
    base_full = jnp.where(root == x_here, base_full, 0.0)
    groups = quarter // cols
    place = home % groups

    up = adapter_up_weight.reshape(kept * rank, quarter)

    def terms(k, slots):
        r = rank_full[:, k * half : (k + 1) * half]
        mine = slots[None, :] == my_slots[:, None]
        spread = jnp.where(mine[:, None, :], r[None, :, :], 0).reshape(kept * rank, half)
        delta = lax.dot_general(
            spread.astype(bf16), up, (((0,), (0,)), ((), ())), preferred_element_type=f32
        ).astype(bf16).astype(f32)
        delta = (adapter_scale * delta).reshape(half, groups, cols)
        b = base_full[k * half : (k + 1) * half][:, None, :]
        at = jnp.arange(groups, dtype=jnp.int32)[None, :, None] == place
        return (delta + jnp.where(at, b, 0.0)).astype(bf16).reshape(half, quarter)

    theirs = swap_cores(terms(1, slot_other))
    ours = terms(0, slot_own)
    both = (ours.astype(f32) + theirs.astype(f32)).astype(bf16)
    got_y = lax.all_to_all(both.reshape(NY, NZ * mine_n, quarter), "y", 0, 0, tiled=True)
    sum_y = jnp.sum(got_y.astype(f32), axis=0).astype(bf16)
    got_z = lax.all_to_all(sum_y.reshape(NZ, mine_n, quarter), "z", 0, 0, tiled=True)
    return jnp.sum(got_z.astype(f32), axis=0).astype(bf16)


def solution(mesh):
    fine = Mesh(np.asarray(mesh.devices).reshape(NZ, NY, NC, NX), ("z", "y", "c", "x"))
    return jax.shard_map(
        local,
        mesh=fine,
        in_specs=(
            P(DP, "x"),
            P(DP, "x"),
            P(DP, "x"),
            P(DP, None, "x"),
            P(DP, None, "x"),
            P(DP),
            P(),
            P(),
            P("x", DP),
            P(DP, "x", None),
            P(DP, None, "x"),
        ),
        out_specs=P(DP, "x"),
        check_vma=False,
    )
```

time: 345 us -> 109 us (0.32)
  waiting for transfers between devices: 286 us -> 19.2 us
  blocking collectives: 15.7 us -> 53 us
  between operations: 13.9 us -> 0.38 us
  starting transfers between devices: 6.93 us -> 15.4 us
    unnamed x4 -> x0, waiting for transfers between devices: 196 us -> none
    all_gather x1 -> x0, waiting for transfers between devices: 80 us -> none  [local(): partial_result = lax.all_gather(attended, 'dp', axis=0, tiled=True)]
    all_to_all x0 -> x3, blocking collectives: none -> 53 us  [the longest x1 20.1 us: local(): lax.all_to_all(jnp.broadcast_to(attended[None], (NZ,) + attended.shape),...]
    psum x1 -> x0, blocking collectives: 15.7 us -> none  [local(): rank_full = lax.psum(rank_local, 'tensor')]
    ppermute x0 -> x8, starting transfers between devices: none -> 10.9 us  [the longest x3 7.24 us: local(): got = lax.ppermute(base_part, ('z', 'x'), pairs)]
    ppermute x0 -> x8, waiting for transfers between devices: none -> 6.28 us  [the longest x3 3.45 us: local(): got = lax.ppermute(base_part, ('z', 'x'), pairs)]
    dot_general x2 -> x4, matrix products: 7.91 us -> 5.66 us  [the longest x2 2.55 us: terms(): lax.dot_general(spread.astype(bf16), up, (((0,), (0,)), ((), ())), prefer...]
  transfers between devices with their start and end apart: 4 -> 9, of which waited for: 3 -> 4; matrix products, arithmetic and copies ran while one was open for 3% -> 4% of each run, Pallas kernels for 0% -> 0%
where the time goes in v1:
time: 109 us; the launch traced here: 107 us
  blocking collectives  53 us (49%)
  waiting for transfers between devices  19.2 us (18%)
  starting transfers between devices  15.4 us (14%)
  matrix products  13.6 us (12%)
  other arithmetic  3.25 us (3%)
  local copies, waits for them, and re-layouts  1.84 us (2%)
    all_to_all x1, blocking collectives, local(): lax.all_to_all(jnp.broadcast_to(attended[None], (NZ,) + attended.shape),...  20.1 us
    all_to_all x1, blocking collectives, local(): lax.all_to_all(both.reshape(NY, NZ * mine_n, quarter), 'y', 0, 0, tiled=T...  18.1 us
    all_to_all x1, blocking collectives, local(): lax.all_to_all(sum_y.reshape(NZ, mine_n, quarter), 'z', 0, 0, tiled=True)  14.8 us
    all_to_all x1, waiting for transfers between devices, local(): lax.all_to_all(jnp.broadcast_to(along_z[None], (NY,) + along_z.shape), 'y...  12.9 us
    ppermute x3, starting transfers between devices, local(): got = lax.ppermute(base_part, ('z', 'x'), pairs)  7.24 us
    all_to_all x1, starting transfers between devices, local(): lax.all_to_all(jnp.broadcast_to(along_z[None], (NY,) + along_z.shape), 'y...  4.46 us
    dot_general x1, matrix products, attend(): jnp.einsum('skgd,sckd->skgc', query4, keys4, preferred_element_type=jnp.f...  3.63 us
    ppermute x3, starting transfers between devices, local(): lax.ppermute(rank_part, 'x', [(i, (i + shift) % NX) for i in range(NX)])  3.61 us
  transfers between devices with their start and end apart: 9, of which 4 were waited for; matrix products, arithmetic and copies ran while one was open for 4% of the time, Pallas kernels for 0%

profile of v1, /device:TPU:6, one launch (start us, length us, event | category | flops | bytes accessed | tf_op | source)
XLA Modules:
  0.0 106.7 jit_solution(1603212118162616548)
XLA Ops:
  0.0 0.8 and_select_fusion
  0.8 0.7 fusion.43
  1.6 0.9 fusion.45
  2.5 0.0 copy-start.5
  2.5 3.6 %fusion.56 = (f32[8,2,8]{2,1,0:T(2,128)S(1)}, f32[8,2,8,1024]{3,2,1,0:T(8,128)S(1)}) fusion(bf16[8,2,8,128]{3,0,2,1:T(8,128)(2,1)} %bitcast.128, pred[8,1024]{1,0:T(8,128)(4,1)S(1)} %fusion.43, bf16[8,1024,256]{2,1,0:T(8,128)(2,1)} %param.14), kind=kOutput, calls=%fused_computation.80 | convolution fusion | flops 33947520 | bytes 4760064 | tf_op jit(solution)/shard_map/skgd,sckd->skgc/dot_general | solution.py:26
  6.1 0.2 fusion.32
  6.4 0.7 fusion.29
  7.2 0.0 copy-start.3
  7.2 0.0 copy-start.4
  7.2 20.1 %all_to_all.20 = bf16[8,8,2048]{2,1,0:T(8,128)(2,1)S(1)} all-to-all(bf16[8,8,2048]{2,1,0:T(8,128)(2,1)S(1)} %broadcast_in_dim.157), channel_id=1, replica_groups=mesh['z'=8,'y'=4,'c'=2,'x'=4] {'z'}, dimensions={0} | all-to-all | bytes 524288 | tf_op jit(solution)/shard_map/all_to_all | solution.py:84
  27.4 1.1 %broadcast_in_dim.159 = bf16[4,64,2048]{2,1,0:T(8,128)(2,1)} broadcast(bf16[64,2048]{1,0:T(8,128)(2,1)S(1)} %bitcast.120), dimensions={1,2} | broadcast | bytes 1310720 | tf_op jit(solution)/shard_map/broadcast_in_dim | solution.py:88
  28.5 4.5 %all-to-all-start.1 = ((bf16[4,64,2048]{2,1,0:T(8,128)(2,1)}), bf16[4,64,2048]{2,1,0:T(8,128)(2,1)S(1)}, u32[]{:S(2)}, u32[]{:S(2)}) async-start(bf16[4,64,2048]{2,1,0:T(8,128)(2,1)} %broadcast_in_dim.159), calls=%async_computation.1 | async-start | bytes 2097152 | tf_op jit(solution)/shard_map/all_to_all | solution.py:87
  32.9 0.2 select_reduce_fusion
  33.2 0.1 reshape.180
  33.4 12.9 %all-to-all-done.1 = bf16[4,64,2048]{2,1,0:T(8,128)(2,1)S(1)} async-done(((bf16[4,64,2048]{2,1,0:T(8,128)(2,1)}), bf16[4,64,2048]{2,1,0:T(8,128)(2,1)S(1)}, u32[]{:S(2)}, u32[]{:S(2)}) %all-to-all-start.1) | async-done | bytes 1048608 | tf_op jit(solution)/shard_map/all_to_all | solution.py:87
  46.2 0.0 collective-permute-start
  46.3 0.1 select_n.85
  46.4 0.1 select_n.90
  46.5 0.1 broadcast_bitcast_fusion
  46.5 0.1 broadcast_compare_fusion.1
  46.6 1.5 %convolution_convert_fusion.1 = bf16[256,128]{1,0:T(8,128)(2,1)S(1)} fusion(bf16[256,2048]{1,0:T(8,128)(2,1)S(1)} %bitcast.116, bf16[2048,128]{1,0:T(8,128)(2,1)} %param.19), kind=kOutput, calls=%fused_computation.25 | convolution fusion | flops 134250496 | bytes 1638400 | tf_op jit(solution)/shard_map/dot_general | solution.py:112
  48.1 0.7 fusion.57
  48.8 0.0 copy-start.1
  48.9 0.2 collective-permute-done
  49.0 2.0 %fusion.58 = f32[256,512]{0,1:S(1)} fusion(bf16[256,2048]{1,0:T(8,128)(2,1)} %collective-permute-done, bf16[2048,512]{0,1:T(8,128)(2,1)S(1)} %bitcast.114), kind=kOutput, calls=%fused_computation.82 | convolution fusion | flops 536870912 | bytes 3670016
  51.0 0.1 select_reduce_fusion.1
  51.1 1.5 %collective-permute-start.1 = (bf16[64,512]{1,0:T(8,128)(2,1)S(1)}, bf16[64,512]{1,0:T(8,128)(2,1)S(1)}, u32[]{:S(2)}, u32[]{:S(2)}) collective-permute-start(bf16[64,512]{1,0:T(8,128)(2,1)S(1)} %pad_maximum_fusion.1), channel_id=1, source_target_pairs={{0,2},{1,3},{2,0},{3,1},{4,6},{5,7},{6,4},{7,5},{8,10},{9,11},{10,... | collective-permute-start | bytes 196616 | tf_op jit(solution)/shard_map/ppermute | solution.py:120
  52.6 2.1 %collective-permute-start.2 = (bf16[64,512]{1,0:T(8,128)(2,1)S(1)}, bf16[64,512]{1,0:T(8,128)(2,1)S(1)}, u32[]{:S(2)}, u32[]{:S(2)}) collective-permute-start(bf16[64,512]{1,0:T(8,128)(2,1)S(1)} %pad_maximum_fusion.1), channel_id=1, source_target_pairs={{0,1},{1,2},{2,3},{3,0},{4,5},{5,6},{6,7},{7,4},{8,9},{9,10},{10,1... | collective-permute-start | bytes 196616 | tf_op jit(solution)/shard_map/ppermute | solution.py:120
  54.7 1.6 %convolution_convert_fusion = bf16[256,128]{1,0:T(8,128)(2,1)S(1)} fusion(bf16[256,2048]{1,0:T(8,128)(2,1)} %collective-permute-done, bf16[2048,128]{1,0:T(8,128)(2,1)S(1)} %copy-done.1), kind=kOutput, calls=%fused_computation.24 | convolution fusion | flops 134250496 | bytes 1638400 | tf_op jit(solution)/shard_map/dot_general | solution.py:113
  56.4 0.0 copy-start.6
  56.4 0.8 collective-permute-start.4
  57.2 5.8 %collective-permute-start.5 = (bf16[512,128]{1,0:T(8,128)(2,1)S(1)}, bf16[512,128]{1,0:T(8,128)(2,1)S(1)}, u32[]{:S(2)}, u32[]{:S(2)}) collective-permute-start(bf16[512,128]{1,0:T(8,128)(2,1)S(1)} %pad_maximum_fusion), channel_id=1, source_target_pairs={{3,0},{35,32},{64,65},{96,97},{129,130},{161,162},{194,195},{226,2... | collective-permute-start | bytes 393224 | tf_op jit(solution)/shard_map/ppermute | solution.py:132
  63.0 0.7 collective-permute-start.6
  63.7 0.0 collective-permute-done.2
  63.7 0.0 collective-permute-done.3
  63.8 0.0 collective-permute-done.4
  63.8 3.4 %collective-permute-done.5 = bf16[512,128]{1,0:T(8,128)(2,1)S(1)} collective-permute-done((bf16[512,128]{1,0:T(8,128)(2,1)S(1)}, bf16[512,128]{1,0:T(8,128)(2,1)S(1)}, u32[]{:S(2)}, u32[]{:S(2)}) %collective-permute-start.5) | collective-permute-done | bytes 131104 | tf_op jit(solution)/shard_map/ppermute | solution.py:132
  67.2 0.1 add_select_fusion
  67.3 0.1 broadcast_in_dim.172
  67.5 1.2 %fusion.14 = bf16[256,2048]{1,0:T(8,128)(2,1)S(1)} fusion(bf16[8,64,2048]{2,1,0:T(8,128)(2,1)S(1)} %copy-done.6, f32[32,8,16,128]{3,2,1,0:T(8,128)S(1)} %bitcast.119, pred[2048]{0:T(1024)(128)(4,1)S(1)} %broadcast_bitcast_fusion, pred[8,256]{1,0:T(8,128)(4,1)S(1)} %get-tuple-element.14, bf16[64,256]{1,0:T(8,128)(2,1)S(1)} %get-tuple-element.8), kind=kOutput, calls=%fused_computation.16 | convolution fusion | flops 540147712 | bytes 5279744 | tf_op jit(solution)/shard_map/dot_general | solution.py:144
  68.7 0.1 collective-permute-start.7
  68.8 2.6 %collective-permute-done.7 = bf16[256,2048]{1,0:T(8,128)(2,1)S(1)} collective-permute-done((bf16[256,2048]{1,0:T(8,128)(2,1)S(1)}, bf16[256,2048]{1,0:T(8,128)(2,1)S(1)}, u32[]{:S(2)}, u32[]{:S(2)}) %collective-permute-start.7) | collective-permute-done | bytes 1048608 | tf_op jit(solution)/shard_map/ppermute | solution.py:52
  71.4 0.1 broadcast_in_dim.168
  71.6 1.3 %add_convert_fusion = bf16[256,2048]{1,0:T(8,128)(2,1)S(1)} fusion(bf16[256,2048]{1,0:T(8,128)(2,1)S(1)} %collective-permute-done.7, f32[32,8,16,128]{3,2,1,0:T(8,128)S(1)} %bitcast.118, bf16[8,64,2048]{2,1,0:T(8,128)(2,1)S(1)} %copy-done.6, pred[2048]{0:T(1024)(128)(4,1)S(1)} %broadcast_bitcast_fusion, pred[8,256]{1,0:T(8,128)(4,1)S(1)} %get-tuple-element.13, ...), kind=kOutput, calls=%fused_computation.21 | convolution fusion | flops 542244864 | bytes 6328320 | tf_op jit(solution)/shard_map/dot_general | solution.py:144
  72.9 18.1 %all_to_all.21 = bf16[4,64,2048]{2,1,0:T(8,128)(2,1)S(1)} all-to-all(bf16[4,64,2048]{2,1,0:T(8,128)(2,1)S(1)} %bitcast.122), channel_id=1, replica_groups=mesh['z'=8,'y'=4,'c'=2,'x'=4] {'y'}, dimensions={0} | all-to-all | bytes 2097152 | tf_op jit(solution)/shard_map/all_to_all | solution.py:155
  91.0 0.2 reduce_sum.64
  91.2 14.8 %all_to_all.22 = bf16[8,8,2048]{2,1,0:T(8,128)(2,1)S(1)} all-to-all(bf16[8,8,2048]{2,1,0:T(8,128)(2,1)S(1)} %bitcast.121), channel_id=1, replica_groups=mesh['z'=8,'y'=4,'c'=2,'x'=4] {'z'}, dimensions={0} | all-to-all | bytes 524288 | tf_op jit(solution)/shard_map/all_to_all | solution.py:157
  106.0 0.7 reduce_sum.65
  (28 shorter events, 0.2 us)
Async XLA Ops:
  0.0 48.1 %copy-start = (bf16[8,2048,64]{1,2,0:T(8,128)(2,1)S(1)}, bf16[8,2048,64]{1,2,0:T(8,128)(2,1)}, u32[]{:S(2)}) copy-start(bf16[8,2048,64]{1,2,0:T(8,128)(2,1)} %param.20) | copy-start | bytes 6291460
  2.5 3.9 %copy-start.2 = (bf16[8,256]{1,0:T(8,128)(2,1)S(1)}, bf16[8,256]{1,0:T(8,128)(2,1)}, u32[]{:S(2)}) copy-start(bf16[8,256]{1,0:T(8,128)(2,1)} %param.13) | copy-start | bytes 12292
  2.5 4.0 %copy-start.5 = (bf16[8,1024,256]{2,1,0:T(8,128)(2,1)S(1)}, bf16[8,1024,256]{2,1,0:T(8,128)(2,1)}, u32[]{:S(2)}) copy-start(bf16[8,1024,256]{2,1,0:T(8,128)(2,1)} %param.15) | copy-start | bytes 12582916
  7.2 25.7 %copy-start.3 = (s32[512]{0:T(512)S(1)}, s32[512]{0:T(512)}, u32[]{:S(2)}) copy-start(s32[512]{0:T(512)} %param.18) | copy-start | bytes 6148
  7.2 25.7 %copy-start.4 = (s32[512]{0:T(512)S(1)}, s32[512]{0:T(512)}, u32[]{:S(2)}) copy-start(s32[512]{0:T(512)} %param.17) | copy-start | bytes 6148
  28.5 17.8 %all-to-all-start.1 = ((bf16[4,64,2048]{2,1,0:T(8,128)(2,1)}), bf16[4,64,2048]{2,1,0:T(8,128)(2,1)S(1)}, u32[]{:S(2)}, u32[]{:S(2)}) async-start(bf16[4,64,2048]{2,1,0:T(8,128)(2,1)} %broadcast_in_dim.159), calls=%async_computation.1 | async-start | bytes 2097152 | tf_op jit(solution)/shard_map/all_to_all | solution.py:87
  46.2 2.8 %collective-permute-start = (bf16[256,2048]{1,0:T(8,128)(2,1)S(1)}, bf16[256,2048]{1,0:T(8,128)(2,1)}, u32[]{:S(2)}, u32[]{:S(2)}) collective-permute-start(bf16[256,2048]{1,0:T(8,128)(2,1)S(1)} %bitcast.115), channel_id=1, source_target_pairs={{0,4},{4,0},{1,5},{5,1},{2,6},{6,2},{3,7},{7,3},{8,12},{12,8},{9,1... | collective-permute-start | bytes 3145736 | tf_op jit(solution)/shard_map/ppermute | solution.py:52
  48.8 5.9 %copy-start.1 = (bf16[2048,128]{1,0:T(8,128)(2,1)S(1)}, bf16[2048,128]{1,0:T(8,128)(2,1)}, u32[]{:S(2)}) copy-start(bf16[2048,128]{1,0:T(8,128)(2,1)} %param.19) | copy-start | bytes 1572868
  51.1 11.9 %collective-permute-start.1 = (bf16[64,512]{1,0:T(8,128)(2,1)S(1)}, bf16[64,512]{1,0:T(8,128)(2,1)S(1)}, u32[]{:S(2)}, u32[]{:S(2)}) collective-permute-start(bf16[64,512]{1,0:T(8,128)(2,1)S(1)} %pad_maximum_fusion.1), channel_id=1, source_target_pairs={{0,2},{1,3},{2,0},{3,1},{4,6},{5,7},{6,4},{7,5},{8,10},{9,11},{10,... | collective-permute-start | bytes 196616 | tf_op jit(solution)/shard_map/ppermute | solution.py:120
  52.6 11.1 %collective-permute-start.2 = (bf16[64,512]{1,0:T(8,128)(2,1)S(1)}, bf16[64,512]{1,0:T(8,128)(2,1)S(1)}, u32[]{:S(2)}, u32[]{:S(2)}) collective-permute-start(bf16[64,512]{1,0:T(8,128)(2,1)S(1)} %pad_maximum_fusion.1), channel_id=1, source_target_pairs={{0,1},{1,2},{2,3},{3,0},{4,5},{5,6},{6,7},{7,4},{8,9},{9,10},{10,1... | collective-permute-start | bytes 196616 | tf_op jit(solution)/shard_map/ppermute | solution.py:120
  54.7 9.0 %collective-permute-start.3 = (bf16[64,512]{1,0:T(8,128)(2,1)S(1)}, bf16[64,512]{1,0:T(8,128)(2,1)S(1)}, u32[]{:S(2)}, u32[]{:S(2)}) collective-permute-start(bf16[64,512]{1,0:T(8,128)(2,1)S(1)} %pad_maximum_fusion.1), channel_id=1, source_target_pairs={{0,3},{1,0},{2,1},{3,2},{4,7},{5,4},{6,5},{7,6},{8,11},{9,8},{10,9... | collective-permute-start | bytes 196616 | tf_op jit(solution)/shard_map/ppermute | solution.py:120
  56.4 11.1 %copy-start.6 = (bf16[8,64,2048]{2,1,0:T(8,128)(2,1)S(1)}, bf16[8,64,2048]{2,1,0:T(8,128)(2,1)}, u32[]{:S(2)}) copy-start(bf16[8,64,2048]{2,1,0:T(8,128)(2,1)} %param.21) | copy-start | bytes 6291460
  56.4 7.4 %collective-permute-start.4 = (bf16[512,128]{1,0:T(8,128)(2,1)S(1)}, bf16[512,128]{1,0:T(8,128)(2,1)S(1)}, u32[]{:S(2)}, u32[]{:S(2)}) collective-permute-start(bf16[512,128]{1,0:T(8,128)(2,1)S(1)} %pad_maximum_fusion), channel_id=1, source_target_pairs={{2,0},{34,32},{67,65},{99,97},{128,130},{160,162},{193,195},{225,2... | collective-permute-start | bytes 393224 | tf_op jit(solution)/shard_map/ppermute | solution.py:132
  57.2 10.0 %collective-permute-start.5 = (bf16[512,128]{1,0:T(8,128)(2,1)S(1)}, bf16[512,128]{1,0:T(8,128)(2,1)S(1)}, u32[]{:S(2)}, u32[]{:S(2)}) collective-permute-start(bf16[512,128]{1,0:T(8,128)(2,1)S(1)} %pad_maximum_fusion), channel_id=1, source_target_pairs={{3,0},{35,32},{64,65},{96,97},{129,130},{161,162},{194,195},{226,2... | collective-permute-start | bytes 393224 | tf_op jit(solution)/shard_map/ppermute | solution.py:132
  63.0 4.2 %collective-permute-start.6 = (bf16[512,128]{1,0:T(8,128)(2,1)S(1)}, bf16[512,128]{1,0:T(8,128)(2,1)S(1)}, u32[]{:S(2)}, u32[]{:S(2)}) collective-permute-start(bf16[512,128]{1,0:T(8,128)(2,1)S(1)} %pad_maximum_fusion), channel_id=1, source_target_pairs={{1,0},{33,32},{66,65},{98,97},{131,130},{163,162},{192,195},{224,2... | collective-permute-start | bytes 393224 | tf_op jit(solution)/shard_map/ppermute | solution.py:132
  68.7 2.7 %collective-permute-start.7 = (bf16[256,2048]{1,0:T(8,128)(2,1)S(1)}, bf16[256,2048]{1,0:T(8,128)(2,1)S(1)}, u32[]{:S(2)}, u32[]{:S(2)}) collective-permute-start(bf16[256,2048]{1,0:T(8,128)(2,1)S(1)} %fusion.14), channel_id=1, source_target_pairs={{0,4},{4,0},{1,5},{5,1},{2,6},{6,2},{3,7},{7,3},{8,12},{12,8},{9,1... | collective-permute-start | bytes 3145736 | tf_op jit(solution)/shard_map/ppermute | solution.py:52

commit v2 on v0

v2 whole, which is shorter than its diff:
```python
import functools

import jax
import jax.numpy as jnp
import numpy as np
from jax import lax
from jax.experimental import pallas as pl
from jax.experimental.pallas import tpu as pltpu
from jax.sharding import Mesh, PartitionSpec as P

HEAD_SIZE = 128
adapter_scale = 0.5
NZ, NY, NC, NX = 8, 4, 2, 4
DP = ("z", "y", "c")
LANES = 128
MIB = 1 << 20
bf16, f32 = jnp.bfloat16, jnp.float32


def in_hbm(*xs):
    return [pltpu.with_memory_space_constraint(x, pltpu.HBM) for x in xs]


def attend_kernel(
    position, query, fresh_key, fresh_value, keys, values,
    out,
    pos, q_buf, fk_buf, fv_buf, k_buf, v_buf,
    q_rows, probs, fresh_part, o_rows, small_sems, sems,
):
    sessions, cache_len, width = keys.shape
    heads_kv = width // HEAD_SIZE
    heads = query.shape[1] // HEAD_SIZE
    group = heads // heads_kv
    small = [
        pltpu.make_async_copy(src, dst, small_sems.at[i])
        for i, (src, dst) in enumerate(
            ((query, q_buf), (position, pos), (fresh_key, fk_buf), (fresh_value, fv_buf))
        )
    ]
    key_copies = [
        pltpu.make_async_copy(keys.at[s], k_buf.at[s], sems.at[0, s]) for s in range(sessions)
    ]
    value_copies = [
        pltpu.make_async_copy(values.at[s], v_buf.at[s], sems.at[1, s]) for s in range(sessions)
    ]
    for copy in small + key_copies:
        copy.start()

    small[0].wait()
    for h in range(heads):
        q_rows[pl.ds(h, sessions, stride=heads), :] = q_buf[
            :, h * HEAD_SIZE : (h + 1) * HEAD_SIZE
        ].astype(f32)
    for copy in small[1:]:
        copy.wait()
    inverse = HEAD_SIZE ** (-0.5)
    rows_all = sessions * heads
    of_row = lax.broadcasted_iota(jnp.int32, (rows_all, 1), 0)
    kv_of_row = (of_row % heads) // group
    wide = jnp.concatenate(
        [jnp.where(kv_of_row == kv, q_rows[...], 0.0) for kv in range(heads_kv)], axis=1
    )
    wide_low = wide.astype(bf16)
    fresh_keys, fresh_values = fk_buf[...].astype(f32), fv_buf[...].astype(f32)
    fresh_key_rows = []
    fresh_value_rows = []
    for s in range(sessions):
        fresh_key_rows.append(jnp.broadcast_to(fresh_keys[s : s + 1, :], (heads, width)))
        fresh_value_rows.append(jnp.broadcast_to(fresh_values[s : s + 1, :], (heads, width)))
    fresh = (
        jnp.sum(wide * jnp.concatenate(fresh_key_rows, axis=0), axis=1, keepdims=True) * inverse
    )
    values_of_rows = jnp.concatenate(fresh_value_rows, axis=0)
    slots = lax.broadcasted_iota(jnp.int32, (1, cache_len), 1)
    batch = sessions // 2
    for g in range(0, sessions, batch):
        for s in range(g, g + batch):
            key_copies[s].wait()
            value_copies[s].start()
        for s in range(g, g + batch):
            rows = slice(s * heads, (s + 1) * heads)
            scores = lax.dot_general(
                wide_low[rows, :], k_buf[s], (((1,), (1,)), ((), ())), preferred_element_type=f32
            )
            live = (slots < pos[s]) & (slots != lax.rem(pos[s], cache_len))
            scores = jnp.where(live, scores * inverse, jnp.float32(-1e30))
            top = jnp.maximum(jnp.max(scores, axis=1, keepdims=True), fresh[rows, :])
            weights = jnp.exp(scores - top)
            fresh_weight = jnp.exp(fresh[rows, :] - top)
            scale = 1.0 / (jnp.sum(weights, axis=1, keepdims=True) + fresh_weight)
            probs[rows, :] = (weights * scale).astype(bf16)
            fresh_part[rows, :] = (fresh_weight * scale).astype(bf16).astype(
                f32
            ) * values_of_rows[rows, :]
    for g in range(0, sessions, batch):
        for s in range(g, g + batch):
            value_copies[s].wait()
        for s in range(g, g + batch):
            rows = slice(s * heads, (s + 1) * heads)
            both = (
                jnp.dot(probs[rows, :], v_buf[s], preferred_element_type=f32) + fresh_part[rows, :]
            )
            for kv in range(heads_kv):
                o_rows[s * heads + kv * group : s * heads + (kv + 1) * group, :] = both[
                    kv * group : (kv + 1) * group, kv * HEAD_SIZE : (kv + 1) * HEAD_SIZE
                ]
    for h in range(heads):
        rounded = o_rows[pl.ds(h, sessions, stride=heads), :].astype(bf16)
        for k in range(out.shape[0]):
            out[k, :, h * HEAD_SIZE : (h + 1) * HEAD_SIZE] = rounded


def attend(query, incoming_key, incoming_value, keys, values, position, repeats):
    sessions, cache_len, width = keys.shape
    features = query.shape[1]
    heads = features // HEAD_SIZE
    columns = sessions * heads
    anywhere = pl.BlockSpec(memory_space=pl.ANY)
    args = (position, query, incoming_key, incoming_value, keys, values)
    return pl.pallas_call(
        attend_kernel,
        out_shape=jax.ShapeDtypeStruct((repeats, sessions, features), bf16),
        in_specs=[anywhere] * 6,
        out_specs=pl.BlockSpec(memory_space=pltpu.VMEM),
        scratch_shapes=[
            pltpu.SMEM((sessions,), jnp.int32),
            pltpu.VMEM((sessions, features), bf16),
            pltpu.VMEM((sessions, width), bf16),
            pltpu.VMEM((sessions, width), bf16),
            pltpu.VMEM((sessions, cache_len, width), bf16),
            pltpu.VMEM((sessions, cache_len, width), bf16),
            pltpu.VMEM((columns, HEAD_SIZE), f32),
            pltpu.VMEM((columns, cache_len), bf16),
            pltpu.VMEM((columns, width), f32),
            pltpu.VMEM((columns, HEAD_SIZE), f32),
            pltpu.SemaphoreType.DMA((4,)),
            pltpu.SemaphoreType.DMA((2, sessions)),
        ],
        compiler_params=pltpu.CompilerParams(vmem_limit_bytes=14 * MIB),
        cost_estimate=pl.CostEstimate(
            flops=4 * columns * cache_len * width,
            bytes_accessed=4 * sessions * cache_len * width,
            transcendentals=columns * cache_len,
        ),
    )(*in_hbm(*args))


def stage_kernel(*refs):
    count = (len(refs) - 2) // 2
    sources, dests, sems = refs[:count], refs[count + 1 : -1], refs[-1]
    copies = [
        pltpu.make_async_copy(src, dst, sems.at[i])
        for i, (src, dst) in enumerate(zip(sources, dests))
    ]
    for copy in copies:
        copy.start()
    for copy in copies:
        copy.wait()


def stage(arrays, after):
    vmem = pl.BlockSpec(memory_space=pltpu.VMEM)
    anywhere = pl.BlockSpec(memory_space=pl.ANY)
    return pl.pallas_call(
        stage_kernel,
        out_shape=tuple(jax.ShapeDtypeStruct(x.shape, x.dtype) for x in arrays),
        in_specs=[anywhere] * (len(arrays) + 1),
        out_specs=(vmem,) * len(arrays),
        scratch_shapes=[pltpu.SemaphoreType.DMA((len(arrays),))],
        compiler_params=pltpu.CompilerParams(vmem_limit_bytes=8 * MIB),
        cost_estimate=pl.CostEstimate(flops=0, bytes_accessed=8 * MIB, transcendentals=0),
    )(*in_hbm(*arrays), after)


def base_kernel(which, p0, pa, pb, w_own, w_other, base_out):
    piece = p0.shape[0]
    cols = w_own.shape[1]
    rows = jnp.concatenate([p0[...], pa[...], pb[...]], axis=0)
    for i, w in enumerate((w_own, w_other)):
        at = pl.ds(pl.multiple_of(which[i] * cols, LANES), cols)
        base_out[:, at] = jnp.dot(rows, w[...], preferred_element_type=f32).astype(bf16)


def base_terms(which, pieces, w_own, w_other):
    count = sum(p.shape[0] for p in pieces)
    cols = w_own.shape[1]
    vmem = pl.BlockSpec(memory_space=pltpu.VMEM)
    return pl.pallas_call(
        base_kernel,
        out_shape=jax.ShapeDtypeStruct((count, 2 * cols), bf16),
        in_specs=[pl.BlockSpec(memory_space=pltpu.SMEM)] + [vmem] * 5,
        out_specs=vmem,
        compiler_params=pltpu.CompilerParams(vmem_limit_bytes=8 * MIB),
        cost_estimate=pl.CostEstimate(
            flops=4 * count * pieces[0].shape[1] * cols, bytes_accessed=2 * MIB, transcendentals=0
        ),
    )(which, *pieces, w_own, w_other)


def rank_kernel(
    first, which, slots, p0, pa, pb, p2, down_own, down_other, w_own, w_other, after, out, rows
):
    piece = p0.shape[0]
    for k, p in enumerate((p0, pa, pb, p2)):
        rows[k * piece : (k + 1) * piece, :] = p[...]
    kept, rank, features = down_own.shape
    cols = w_own.shape[1]
    acc = jnp.zeros((rank, slots.shape[1]), f32)
    for i, down in enumerate((down_own, down_other)):
        portion = lax.dot_general(
            down[...].reshape(kept * rank, features),
            rows[...],
            (((1,), (1,)), ((), ())),
            preferred_element_type=f32,
        )
        for j in range(kept):
            acc = acc + jnp.where(
                slots[...] == first[i] + j, portion[j * rank : (j + 1) * rank, :], 0.0
            )
    out[:rank, :] = acc.astype(bf16)
    for i, w in enumerate((w_own, w_other)):
        at = pl.ds(pl.multiple_of(which[i] * cols, LANES), cols)
        out[rank:, at] = jnp.dot(p2[...], w[...], preferred_element_type=f32).astype(bf16)


def rank_terms(first, which, slots, pieces, down_own, down_other, w_own, w_other, after):
    count = slots.shape[1]
    piece, features = pieces[0].shape
    kept, rank, features = down_own.shape
    vmem = pl.BlockSpec(memory_space=pltpu.VMEM)
    smem = pl.BlockSpec(memory_space=pltpu.SMEM)
    return pl.pallas_call(
        rank_kernel,
        out_shape=jax.ShapeDtypeStruct((rank + piece, count), bf16),
        in_specs=[smem, smem] + [vmem] * 9 + [pl.BlockSpec(memory_space=pl.ANY)],
        out_specs=vmem,
        scratch_shapes=[pltpu.VMEM((count, features), bf16)],
        compiler_params=pltpu.CompilerParams(vmem_limit_bytes=12 * MIB),
        cost_estimate=pl.CostEstimate(
            flops=4 * count * features * kept * rank, bytes_accessed=6 * MIB, transcendentals=0
        ),
    )(first, which, slots, *pieces, down_own, down_other, w_own, w_other, after)


def expand_kernel(first, slots, r0, r1, r2, r3, up_own, up_other, o0, oa, ob, o2, spread):
    outs = (o0, oa, ob, o2)
    count = slots.shape[1]
    kept_rank, quarter = up_own.shape
    piece = o0.shape[0]
    rank = r0.shape[0] - piece
    summed = (r0[...].astype(f32) + r1[...].astype(f32)) + (
        r2[...].astype(f32) + r3[...].astype(f32)
    )
    ranks = summed[:rank, :].T
    both = jnp.concatenate([ranks, ranks], axis=1)
    slot_rows = jnp.broadcast_to(slots[...].astype(f32), (LANES, count)).T
    part = lax.broadcasted_iota(jnp.int32, (1, LANES), 1) // rank
    for which in range(2):
        for j in range(kept_rank // LANES):
            slot = (first[which] + 2 * j + part).astype(f32)
            at = which * kept_rank + j * LANES
            spread[:, at : at + LANES] = jnp.where(slot_rows == slot, both, 0.0).astype(bf16)
    step = 512
    for n in range(0, quarter, step):
        cols = slice(n, n + step)
        delta = jnp.dot(
            spread[:, :kept_rank], up_own[:, cols], preferred_element_type=f32
        ) + jnp.dot(spread[:, kept_rank:], up_other[:, cols], preferred_element_type=f32)
        delta = (adapter_scale * delta.astype(bf16).astype(f32)).astype(bf16)
        for k, o in enumerate(outs):
            o[:, cols] = delta[k * piece : (k + 1) * piece, :]

    @pl.when(first[3] == 1)
    def _():
        at = pl.ds(pl.multiple_of(first[2], LANES), count)
        o2[:, at] = (o2[:, at].astype(f32) + summed[rank:, :]).astype(bf16)


def expand(first, slots, ranks, up_own, up_other):
    count = slots.shape[1]
    kept_rank, quarter = up_own.shape
    piece = count // NY
    vmem = pl.BlockSpec(memory_space=pltpu.VMEM)
    smem = pl.BlockSpec(memory_space=pltpu.SMEM)
    return pl.pallas_call(
        expand_kernel,
        out_shape=(jax.ShapeDtypeStruct((piece, quarter), bf16),) * 4,
        in_specs=[smem] + [vmem] * 7,
        out_specs=(vmem,) * 4,
        scratch_shapes=[pltpu.VMEM((count, 2 * kept_rank), bf16)],
        compiler_params=pltpu.CompilerParams(vmem_limit_bytes=12 * MIB),
        cost_estimate=pl.CostEstimate(
            flops=4 * count * kept_rank * quarter, bytes_accessed=6 * MIB, transcendentals=0
        ),
    )(first, slots, *ranks, up_own, up_other)


def join_kernel(place, d0, ea, eb, b0, b1, b2, out):
    out[...] = ((d0[...].astype(f32) + ea[...].astype(f32)) + eb[...].astype(f32)).astype(bf16)

    @pl.when(place[3] == 1)
    def _():
        cols = b0.shape[1]
        for i, b in enumerate((b0, b1, b2)):
            at = pl.ds(pl.multiple_of(place[i], LANES), cols)
            total = (d0[:, at].astype(f32) + ea[:, at].astype(f32)) + eb[:, at].astype(f32)
            out[:, at] = (total + b[...].astype(f32)).astype(bf16)


def join(place, rows, bases):
    vmem = pl.BlockSpec(memory_space=pltpu.VMEM)
    return pl.pallas_call(
        join_kernel,
        out_shape=jax.ShapeDtypeStruct(rows[0].shape, bf16),
        in_specs=[pl.BlockSpec(memory_space=pltpu.SMEM)] + [vmem] * 6,
        out_specs=vmem,
        compiler_params=pltpu.CompilerParams(vmem_limit_bytes=8 * MIB),
        cost_estimate=pl.CostEstimate(flops=MIB, bytes_accessed=MIB, transcendentals=0),
    )(place, *rows, *bases)


def swap_cores(x):
    return lax.ppermute(x, "c", [(0, 1), (1, 0)])


def along_y(x, way):
    pairs = []
    for y in range(NY):
        for c in range(NC):
            step = way if c == 0 else -way
            pairs.append((y * NC + c, ((y + step) % NY) * NC + c))
    return lax.ppermute(x, ("y", "c"), pairs)


def to_root(x, shift):
    pairs = []
    for z in range(NZ):
        owner = z // (NZ // NX)
        pairs.append((z * NX + (owner - shift) % NX, z * NX + owner))
    return lax.ppermute(x, ("z", "x"), pairs)


def along_x(x, shift):
    return lax.ppermute(x, "x", [(i, (i + shift) % NX) for i in range(NX)])


def local(
    query,
    incoming_key,
    incoming_value,
    cycle_key_cache,
    cycle_value_cache,
    position,
    tenant,
    tenant_adapter_index,
    output_weight,
    adapter_down_weight,
    adapter_up_weight,
):
    kept, features, rank = adapter_down_weight.shape
    cols = output_weight.shape[1]
    quarter = adapter_up_weight.shape[2]
    mine_n = query.shape[0]
    block = NZ * mine_n
    z_here, y_here, core, x_here = (lax.axis_index(a) for a in ("z", "y", "c", "x"))
    home = (z_here * NY + y_here) * NC + core
    other = home + 1 - 2 * core
    down = jnp.swapaxes(adapter_down_weight, 1, 2)
    up = adapter_up_weight.reshape(kept * rank, quarter)

    copies = attend(
        query,
        incoming_key,
        incoming_value,
        cycle_key_cache,
        cycle_value_cache,
        position,
        NZ,
    )
    copies, down, up, output_weight = lax.optimization_barrier((copies, down, up, output_weight))
    down_other = swap_cores(down)
    w_other = swap_cores(output_weight)
    up_other = swap_cores(up)
    p0 = lax.all_to_all(copies, "z", 0, 0, tiled=True).reshape(block, features)

    pa = along_y(p0, 1)
    pb = along_y(p0, -1)
    p2 = along_y(pa, 1)

    tenants_all = tenant_adapter_index.shape[0]
    matches = tenant[:, None] == jnp.arange(tenants_all, dtype=jnp.int32)[None, :]
    slot_of = jnp.sum(jnp.where(matches, tenant_adapter_index[None, :], 0), axis=1)
    table = slot_of.reshape(NZ, NY, NC, mine_n).transpose(2, 1, 0, 3).reshape(NC * NY, block)
    ahead = 1 - 2 * core
    ys = jnp.stack([y_here, y_here - ahead, y_here + ahead, y_here + 2]) % NY
    pick = (ys + core * NY)[:, None] == jnp.arange(NC * NY, dtype=jnp.int32)[None, :]
    slots = jnp.sum(jnp.where(pick[:, :, None], table[None], 0), axis=1).reshape(1, NY * block)

    add = lambda *xs: functools.reduce(jnp.add, [x.astype(f32) for x in xs]).astype(bf16)
    is_root = (x_here == z_here // (NZ // NX)).astype(jnp.int32)
    width = NC * cols
    columns = (z_here % (NZ // NX)) * NY
    which = jnp.stack([core, 1 - core])
    first = jnp.stack([home * kept, other * kept, (columns + y_here) * width, is_root])

    (down_other,) = stage((down_other,), p0)
    base_part = base_terms(which, (p0, pa, pb), output_weight, w_other)
    sums = [base_part] + [to_root(base_part, s) for s in (2, 1, 3)]
    packed = rank_terms(
        first, which, slots, (p0, pa, pb, p2), down, down_other, output_weight, w_other, base_part
    )
    packs = [packed] + [along_x(packed, s) for s in (1, 3, 2)]
    base = add(*sums).reshape(NY - 1, block, width)
    bases = [base[0], along_y(base[1], -1), along_y(base[2], 1)]
    senders = jnp.stack([y_here, y_here + ahead, y_here - ahead]) % NY
    place = jnp.concatenate([(columns + senders) * width, is_root[None]])

    ups = stage((up, up_other), packed)
    d0, da, db, d2 = expand(first, slots, packs, *ups)

    e2 = along_y(d2, 1)
    ea = along_y(da, -1)
    eb = along_y(add(db, e2), 1)
    home_rows = join(place, (d0, ea, eb), bases)
    got = lax.all_to_all(home_rows.reshape(NZ, mine_n, quarter), "z", 0, 0, tiled=True)
    return jnp.sum(got.astype(f32), axis=0).astype(bf16)


def solution(mesh):
    fine = Mesh(np.asarray(mesh.devices).reshape(NZ, NY, NC, NX), DP + ("x",))
    return jax.shard_map(
        local,
        mesh=fine,
        in_specs=(
            P(DP, "x"),
            P(DP, "x"),
            P(DP, "x"),
            P(DP, None, "x"),
            P(DP, None, "x"),
            P(DP),
            P(),
            P(),
            P("x", DP),
            P(DP, "x", None),
            P(DP, None, "x"),
        ),
        out_specs=P(DP, "x"),
        check_vma=False,
    )
```

time: 345 us -> 93.1 us (0.27)
  waiting for transfers between devices: 286 us -> 31.1 us
  starting transfers between devices: 6.93 us -> 29.3 us
  Pallas kernels: 0 us -> 16.6 us
  matrix products: 15.9 us -> 0 us
  between operations: 13.9 us -> 0.29 us
    unnamed x4 -> x0, waiting for transfers between devices: 196 us -> none
    all_gather x1 -> x0, waiting for transfers between devices: 80 us -> none  [local(): partial_result = lax.all_gather(attended, 'dp', axis=0, tiled=True)]
    ppermute x0 -> x17, starting transfers between devices: none -> 20.8 us  [the longest x8 10.7 us: along_y(): return lax.ppermute(x, ('y', 'c'), pairs)]
    ppermute x0 -> x17, waiting for transfers between devices: none -> 19.3 us  [the longest x8 19.3 us: along_y(): return lax.ppermute(x, ('y', 'c'), pairs)]
    pallas_call x0 -> x7, Pallas kernels: none -> 16.6 us  [the longest x1 5.91 us: attend(): pl.pallas_call(attend_kernel, out_shape=jax.ShapeDtypeStruct((repeats, se...]
    psum x1 -> x0, blocking collectives: 15.7 us -> none  [local(): rank_full = lax.psum(rank_local, 'tensor')]
    dot_general x5 -> x0, matrix products: 13 us -> none  [the longest x1 4.87 us: local(): jnp.dot(rank_spread, adapter_up_weight.reshape(kept_state * rank_extent,...]
    all_to_all x0 -> x1, blocking collectives: none -> 12.9 us  [local(): lax.all_to_all(home_rows.reshape(NZ, mine_n, quarter), 'z', 0, 0, tiled=T...]
  transfers between devices with their start and end apart: 4 -> 18, of which waited for: 3 -> 6; matrix products, arithmetic and copies ran while one was open for 3% -> 1% of each run, Pallas kernels for 0% -> 11%
where the time goes in v2:
time: 93.1 us; the launch traced here: 92.1 us
  waiting for transfers between devices  31.1 us (33%)
  starting transfers between devices  29.3 us (31%)
  Pallas kernels  16.6 us (18%)
  blocking collectives  12.9 us (14%)
  other arithmetic  1.58 us (2%)
    ppermute x8, waiting for transfers between devices, along_y(): return lax.ppermute(x, ('y', 'c'), pairs)  19.3 us
    all_to_all x1, blocking collectives, local(): lax.all_to_all(home_rows.reshape(NZ, mine_n, quarter), 'z', 0, 0, tiled=T...  12.9 us
    all_to_all x1, waiting for transfers between devices, local(): p0 = lax.all_to_all(copies, 'z', 0, 0, tiled=True).reshape(block, features)  11.8 us
    ppermute x8, starting transfers between devices, along_y(): return lax.ppermute(x, ('y', 'c'), pairs)  10.7 us
    all_to_all x1, starting transfers between devices, local(): p0 = lax.all_to_all(copies, 'z', 0, 0, tiled=True).reshape(block, features)  8.47 us
    ppermute x3, starting transfers between devices, to_root(): return lax.ppermute(x, ('z', 'x'), pairs)  5.95 us
    pallas_call x1, Pallas kernels, attend(): pl.pallas_call(attend_kernel, out_shape=jax.ShapeDtypeStruct((repeats, se...  5.91 us
    pallas_call x2, Pallas kernels, stage(): pl.pallas_call(stage_kernel, out_shape=tuple((jax.ShapeDtypeStruct(x.shap...  3.84 us
  transfers between devices with their start and end apart: 18, of which 6 were waited for; matrix products, arithmetic and copies ran while one was open for 1% of the time, Pallas kernels for 11%

profile of v2, /device:TPU:6, one launch (start us, length us, event | category | flops | bytes accessed | tf_op | source)
XLA Modules:
  0.0 92.1 jit_solution(5820646096023737928)
XLA Ops:
  0.0 5.9 %shard_map.109 = bf16[8,8,2048]{2,1,0:T(8,128)(2,1)} custom-call(s32[8]{0:T(128)} %position.1, bf16[8,2048]{1,0:T(8,128)(2,1)} %query.1, bf16[8,256]{1,0:T(8,128)(2,1)} %fresh_key.1, bf16[8,256]{1,0:T(8,128)(2,1)} %fresh_value.1, bf16[8,1024,256]{2,1,0:T(8,128)(2,1)} %keys.1, bf16[8,1024,256]{2,1,0:T(8,128)(2,1)} %values.1), custom_call_target="tpu_custom_call" | custom-call | flops 134217728 | bytes 8388608 | tf_op jit(solution)/shard_map/pallas_call | solution.py:120
  5.9 0.1 collective-permute-start.3
  6.0 0.5 collective-permute-start.8
  6.5 8.5 %all-to-all-start = ((bf16[8,8,2048]{2,1,0:T(8,128)(2,1)}), bf16[8,8,2048]{2,1,0:T(8,128)(2,1)S(1)}, u32[]{:S(2)}, u32[]{:S(2)}) async-start(bf16[8,8,2048]{2,1,0:T(8,128)(2,1)} %shard_map.109), calls=%async_computation | async-start | bytes 524288 | tf_op jit(solution)/shard_map/all_to_all | solution.py:384
  15.0 0.1 collective-permute-start.4
  15.1 0.2 select_reduce_fusion
  15.4 11.8 %all-to-all-done = bf16[8,8,2048]{2,1,0:T(8,128)(2,1)S(1)} async-done(((bf16[8,8,2048]{2,1,0:T(8,128)(2,1)}), bf16[8,8,2048]{2,1,0:T(8,128)(2,1)S(1)}, u32[]{:S(2)}, u32[]{:S(2)}) %all-to-all-start) | async-done | bytes 262176 | tf_op jit(solution)/shard_map/all_to_all | solution.py:384
  27.2 1.6 %collective-permute-start = (bf16[64,2048]{1,0:T(8,128)(2,1)S(1)}, bf16[64,2048]{1,0:T(8,128)(2,1)}, u32[]{:S(2)}, u32[]{:S(2)}) collective-permute-start(bf16[64,2048]{1,0:T(8,128)(2,1)S(1)} %bitcast.17), channel_id=1, source_target_pairs={{0,8},{4,28},{8,16},{12,4},{16,24},{20,12},{24,0},{28,20},{1,9},{5... | collective-permute-start | bytes 786440 | tf_op jit(solution)/shard_map/ppermute | solution.py:332
  28.7 0.1 fusion.2
  28.8 0.1 reshape.137
  28.9 0.1 broadcast_in_dim.51
  29.0 0.1 iota_compare_fusion.1
  29.1 1.7 %collective-permute-start.1 = (bf16[64,2048]{1,0:T(8,128)(2,1)S(1)}, bf16[64,2048]{1,0:T(8,128)(2,1)}, u32[]{:S(2)}, u32[]{:S(2)}) collective-permute-start(bf16[64,2048]{1,0:T(8,128)(2,1)S(1)} %bitcast.18), channel_id=1, source_target_pairs={{0,24},{4,12},{8,0},{12,20},{16,8},{20,28},{24,16},{28,4},{1,25},{... | collective-permute-start | bytes 786440 | tf_op jit(solution)/shard_map/ppermute | solution.py:332
  30.8 6.2 %collective-permute-done.pa = bf16[64,2048]{1,0:T(8,128)(2,1)} collective-permute-done((bf16[64,2048]{1,0:T(8,128)(2,1)S(1)}, bf16[64,2048]{1,0:T(8,128)(2,1)}, u32[]{:S(2)}, u32[]{:S(2)}) %collective-permute-start) | collective-permute-done | bytes 262176 | tf_op jit(solution)/shard_map/ppermute | solution.py:332
  37.0 0.5 collective-permute-start.2
  37.5 0.1 select_reduce_fusion.1
  37.6 0.1 reshape.138.slots
  37.7 0.1 pad_add_fusion.1.which
  37.7 0.1 add_add_fusion.first
  37.8 0.0 collective-permute-done.4.w_other
  37.8 0.0 collective-permute-done.1.pb
  37.8 1.6 %shard_map.111.after = bf16[192,256]{1,0:T(8,128)(2,1)S(1)} custom-call(s32[2]{0:T(128)S(1)} %pad_add_fusion.1.which, bf16[64,2048]{1,0:T(8,128)(2,1)S(1)} %bitcast.19, bf16[64,2048]{1,0:T(8,128)(2,1)} %collective-permute-done.pa, bf16[64,2048]{1,0:T(8,128)(2,1)} %collective-permute-done.1.pb, bf16[2048,128]{1,0:T(8,128)(2,1)S(1)} %copy-done.1, ...), custom_call_target="tpu_custom_call" | custom-call | flops 201326592 | bytes 2097152 | tf_op jit(solution)/shard_map/pallas_call | solution.py:188
  39.4 0.0 collective-permute-done.3.refs_0_
  39.4 1.6 %shard_map.110.down_other = bf16[8,64,2048]{2,1,0:T(8,128)(2,1)S(1)} custom-call(bf16[8,64,2048]{2,1,0:T(8,128)(2,1)} %collective-permute-done.3.refs_0_, bf16[64,2048]{1,0:T(8,128)(2,1)S(1)} %bitcast.20), custom_call_target="tpu_custom_call" | custom-call | bytes 8388608 | tf_op jit(solution)/shard_map/pallas_call | solution.py:164
  41.0 3.8 %collective-permute-done.2.p2 = bf16[64,2048]{1,0:T(8,128)(2,1)} collective-permute-done((bf16[64,2048]{1,0:T(8,128)(2,1)}, bf16[64,2048]{1,0:T(8,128)(2,1)}, u32[]{:S(2)}, u32[]{:S(2)}) %collective-permute-start.2) | collective-permute-done | bytes 262176 | tf_op jit(solution)/shard_map/ppermute | solution.py:332
  44.9 2.6 %shard_map.112.refs_2_.r0 = bf16[128,256]{1,0:T(8,128)(2,1)S(1)} custom-call(s32[4]{0:T(128)S(1)} %add_add_fusion.first, s32[2]{0:T(128)S(1)} %pad_add_fusion.1.which, s32[1,256]{1,0:T(1,128)S(1)} %reshape.138.slots, bf16[64,2048]{1,0:T(8,128)(2,1)S(1)} %bitcast.21, bf16[64,2048]{1,0:T(8,128)(2,1)} %collective-permute-done.pa, ...), custom_call_target="tpu_custom_call" | custom-call | flops 1073741824 | bytes 6291456 | tf_op jit(solution)/shard_map/pallas_call | solution.py:232
  47.4 0.6 collective-permute-start.5
  48.0 1.5 %collective-permute-start.6 = (bf16[128,256]{1,0:T(8,128)(2,1)S(1)}, bf16[128,256]{1,0:T(8,128)(2,1)S(1)}, u32[]{:S(2)}, u32[]{:S(2)}) collective-permute-start(bf16[128,256]{1,0:T(8,128)(2,1)S(1)} %shard_map.112.refs_2_.r0), channel_id=1, source_target_pairs={{0,3},{1,0},{2,1},{3,2},{4,7},{5,4},{6,5},{7,6},{8,11},{9,8},{10,9... | collective-permute-start | bytes 196616 | tf_op jit(solution)/shard_map/ppermute | solution.py:344
  49.5 1.4 %collective-permute-start.7 = (bf16[128,256]{1,0:T(8,128)(2,1)S(1)}, bf16[128,256]{1,0:T(8,128)(2,1)S(1)}, u32[]{:S(2)}, u32[]{:S(2)}) collective-permute-start(bf16[128,256]{1,0:T(8,128)(2,1)S(1)} %shard_map.112.refs_2_.r0), channel_id=1, source_target_pairs={{0,2},{1,3},{2,0},{3,1},{4,6},{5,7},{6,4},{7,5},{8,10},{9,11},{10,... | collective-permute-start | bytes 196616 | tf_op jit(solution)/shard_map/ppermute | solution.py:344
  50.9 0.7 collective-permute-start.12
  51.6 4.6 %collective-permute-start.13 = (bf16[192,256]{1,0:T(8,128)(2,1)S(1)}, bf16[192,256]{1,0:T(8,128)(2,1)S(1)}, u32[]{:S(2)}, u32[]{:S(2)}) collective-permute-start(bf16[192,256]{1,0:T(8,128)(2,1)S(1)} %shard_map.111.after), channel_id=1, source_target_pairs={{3,0},{35,32},{64,65},{96,97},{129,130},{161,162},{194,195},{226,2... | collective-permute-start | bytes 294920 | tf_op jit(solution)/shard_map/ppermute | solution.py:340
  56.2 2.2 %shard_map.113 = (bf16[512,2048]{1,0:T(8,128)(2,1)S(1)}, bf16[512,2048]{1,0:T(8,128)(2,1)S(1)}) custom-call(bf16[512,2048]{1,0:T(8,128)(2,1)} %bitcast.12.refs_0_, bf16[512,2048]{1,0:T(8,128)(2,1)} %collective-permute-done.8.refs_1_, bf16[128,256]{1,0:T(8,128)(2,1)S(1)} %shard_map.112.refs_2_.r0), custom_call_target="tpu_custom_call" | custom-call | bytes 8388608 | tf_op jit(solution)/shard_map/pallas_call | solution.py:164
  58.5 0.7 collective-permute-start.14
  59.2 2.1 %shard_map.114 = (bf16[64,2048]{1,0:T(8,128)(2,1)S(1)}, bf16[64,2048]{1,0:T(8,128)(2,1)S(1)}, bf16[64,2048]{1,0:T(8,128)(2,1)S(1)}, bf16[64,2048]{1,0:T(8,128)(2,1)S(1)}) custom-call(s32[4]{0:T(128)S(1)} %add_add_fusion.first, s32[1,256]{1,0:T(1,128)S(1)} %reshape.138.slots, bf16[128,256]{1,0:T(8,128)(2,1)S(1)} %shard_map.112.refs_2_.r0, ...), custom_call_target="tpu_custom_call" | custom-call | flops 1073741824 | bytes 6291456 | tf_op jit(solution)/shard_map/pallas_call | solution.py:285
  61.3 0.1 collective-permute-start.10
  61.4 0.1 fusion.1
  61.5 0.1 add_convert_fusion.1
  61.6 3.5 %collective-permute-start.9 = (bf16[64,2048]{1,0:T(8,128)(2,1)S(1)}, bf16[64,2048]{1,0:T(8,128)(2,1)S(1)}, u32[]{:S(2)}, u32[]{:S(2)}) collective-permute-start(bf16[64,2048]{1,0:T(8,128)(2,1)S(1)} %get-tuple-element.22), channel_id=1, source_target_pairs={{0,24},{4,12},{8,0},{12,20},{16,8},{20,28},{24,16},{28,4},{1,25},{... | collective-permute-start | bytes 786440 | tf_op jit(solution)/shard_map/ppermute | solution.py:332
  65.0 4.3 %collective-permute-done.10 = bf16[64,2048]{1,0:T(8,128)(2,1)S(1)} collective-permute-done((bf16[64,2048]{1,0:T(8,128)(2,1)S(1)}, bf16[64,2048]{1,0:T(8,128)(2,1)S(1)}, u32[]{:S(2)}, u32[]{:S(2)}) %collective-permute-start.10) | collective-permute-done | bytes 262176 | tf_op jit(solution)/shard_map/ppermute | solution.py:332
  69.3 0.1 add_convert_fusion
  69.4 0.1 collective-permute-start.11
  69.5 3.3 %collective-permute-start.15 = (bf16[64,256]{1,0:T(8,128)(2,1)S(1)}, bf16[64,256]{1,0:T(8,128)(2,1)S(1)}, u32[]{:S(2)}, u32[]{:S(2)}) collective-permute-start(bf16[64,256]{1,0:T(8,128)(2,1)S(1)} %get-tuple-element.26), channel_id=1, source_target_pairs={{0,24},{4,12},{8,0},{12,20},{16,8},{20,28},{24,16},{28,4},{1,25},{... | collective-permute-start | bytes 98312 | tf_op jit(solution)/shard_map/ppermute | solution.py:332
  72.8 0.1 pad_add_fusion.place
  72.8 1.5 %collective-permute-done.15.b1 = bf16[64,256]{1,0:T(8,128)(2,1)S(1)} collective-permute-done((bf16[64,256]{1,0:T(8,128)(2,1)S(1)}, bf16[64,256]{1,0:T(8,128)(2,1)S(1)}, u32[]{:S(2)}, u32[]{:S(2)}) %collective-permute-start.15) | collective-permute-done | bytes 32800 | tf_op jit(solution)/shard_map/ppermute | solution.py:332
  74.4 3.5 %collective-permute-done.16.b2 = bf16[64,256]{1,0:T(8,128)(2,1)S(1)} collective-permute-done((bf16[64,256]{1,0:T(8,128)(2,1)S(1)}, bf16[64,256]{1,0:T(8,128)(2,1)S(1)}, u32[]{:S(2)}, u32[]{:S(2)}) %collective-permute-start.16) | collective-permute-done | bytes 32800 | tf_op jit(solution)/shard_map/ppermute | solution.py:332
  77.9 0.6 shard_map.115
  78.5 12.9 %all_to_all.10 = bf16[8,8,2048]{2,1,0:T(8,128)(2,1)S(1)} all-to-all(bf16[8,8,2048]{2,1,0:T(8,128)(2,1)S(1)} %bitcast.24), channel_id=1, replica_groups=mesh['z'=8,'y'=4,'c'=2,'x'=4] {'z'}, dimensions={0} | all-to-all | bytes 524288 | tf_op jit(solution)/shard_map/all_to_all | solution.py:425
  91.4 0.7 reduce_sum.32
  (20 shorter events, 0.1 us)
Async XLA Ops:
  0.0 5.9 %copy-start = (bf16[8,2048,64]{1,2,0:T(8,128)(2,1)S(1)}, bf16[8,2048,64]{1,2,0:T(8,128)(2,1)}, u32[]{:S(2)}) copy-start(bf16[8,2048,64]{1,2,0:T(8,128)(2,1)} %param.20) | copy-start | bytes 6291460
  0.0 15.0 %copy-start.1 = (bf16[2048,128]{1,0:T(8,128)(2,1)S(1)}, bf16[2048,128]{1,0:T(8,128)(2,1)}, u32[]{:S(2)}) copy-start(bf16[2048,128]{1,0:T(8,128)(2,1)} %w_own.1) | copy-start | bytes 1572868
  0.0 15.1 %copy-start.3 = (s32[512]{0:T(512)S(1)}, s32[512]{0:T(512)}, u32[]{:S(2)}) copy-start(s32[512]{0:T(512)} %param.17) | copy-start | bytes 6148
  0.0 15.1 %copy-start.2 = (s32[512]{0:T(512)S(1)}, s32[512]{0:T(512)}, u32[]{:S(2)}) copy-start(s32[512]{0:T(512)} %param.18) | copy-start | bytes 6148
  5.9 33.5 %collective-permute-start.3 = (bf16[8,64,2048]{2,1,0:T(8,128)(2,1)S(1)}, bf16[8,64,2048]{2,1,0:T(8,128)(2,1)}, u32[]{:S(2)}, u32[]{:S(2)}) collective-permute-start(bf16[8,64,2048]{2,1,0:T(8,128)(2,1)S(1)} %bitcast.22), channel_id=1, source_target_pairs={{0,4},{4,0},{1,5},{5,1},{2,6},{6,2},{3,7},{7,3},{8,12},{12,8},{9,1... | collective-permute-start | bytes 6291464 | tf_op jit(solution)/shard_map/ppermute | solution.py:323
  6.0 45.5 %collective-permute-start.8 = (bf16[512,2048]{1,0:T(8,128)(2,1)}, bf16[512,2048]{1,0:T(8,128)(2,1)}, u32[]{:S(2)}, u32[]{:S(2)}) collective-permute-start(bf16[512,2048]{1,0:T(8,128)(2,1)} %bitcast.12.refs_0_), channel_id=1, source_target_pairs={{0,4},{4,0},{1,5},{5,1},{2,6},{6,2},{3,7},{7,3},{8,12},{12,8},{9,1... | collective-permute-start | bytes 6291464 | tf_op jit(solution)/shard_map/ppermute | solution.py:323
  6.5 20.6 %all-to-all-start = ((bf16[8,8,2048]{2,1,0:T(8,128)(2,1)}), bf16[8,8,2048]{2,1,0:T(8,128)(2,1)S(1)}, u32[]{:S(2)}, u32[]{:S(2)}) async-start(bf16[8,8,2048]{2,1,0:T(8,128)(2,1)} %shard_map.109), calls=%async_computation | async-start | bytes 524288 | tf_op jit(solution)/shard_map/all_to_all | solution.py:384
  15.0 22.8 %collective-permute-start.4 = (bf16[2048,128]{1,0:T(8,128)(2,1)S(1)}, bf16[2048,128]{1,0:T(8,128)(2,1)S(1)}, u32[]{:S(2)}, u32[]{:S(2)}) collective-permute-start(bf16[2048,128]{1,0:T(8,128)(2,1)S(1)} %copy-done.1), channel_id=1, source_target_pairs={{0,4},{4,0},{1,5},{5,1},{2,6},{6,2},{3,7},{7,3},{8,12},{12,8},{9,1... | collective-permute-start | bytes 1572872 | tf_op jit(solution)/shard_map/ppermute | solution.py:323
  27.2 9.8 %collective-permute-start = (bf16[64,2048]{1,0:T(8,128)(2,1)S(1)}, bf16[64,2048]{1,0:T(8,128)(2,1)}, u32[]{:S(2)}, u32[]{:S(2)}) collective-permute-start(bf16[64,2048]{1,0:T(8,128)(2,1)S(1)} %bitcast.17), channel_id=1, source_target_pairs={{0,8},{4,28},{8,16},{12,4},{16,24},{20,12},{24,0},{28,20},{1,9},{5... | collective-permute-start | bytes 786440 | tf_op jit(solution)/shard_map/ppermute | solution.py:332
  29.1 8.7 %collective-permute-start.1 = (bf16[64,2048]{1,0:T(8,128)(2,1)S(1)}, bf16[64,2048]{1,0:T(8,128)(2,1)}, u32[]{:S(2)}, u32[]{:S(2)}) collective-permute-start(bf16[64,2048]{1,0:T(8,128)(2,1)S(1)} %bitcast.18), channel_id=1, source_target_pairs={{0,24},{4,12},{8,0},{12,20},{16,8},{20,28},{24,16},{28,4},{1,25},{... | collective-permute-start | bytes 786440 | tf_op jit(solution)/shard_map/ppermute | solution.py:332
  37.0 7.9 %collective-permute-start.2 = (bf16[64,2048]{1,0:T(8,128)(2,1)}, bf16[64,2048]{1,0:T(8,128)(2,1)}, u32[]{:S(2)}, u32[]{:S(2)}) collective-permute-start(bf16[64,2048]{1,0:T(8,128)(2,1)} %collective-permute-done.pa), channel_id=1, source_target_pairs={{0,8},{4,28},{8,16},{12,4},{16,24},{20,12},{24,0},{28,20},{1,9},{5... | collective-permute-start | bytes 786440 | tf_op jit(solution)/shard_map/ppermute | solution.py:332
  47.4 11.1 %collective-permute-start.5 = (bf16[128,256]{1,0:T(8,128)(2,1)S(1)}, bf16[128,256]{1,0:T(8,128)(2,1)S(1)}, u32[]{:S(2)}, u32[]{:S(2)}) collective-permute-start(bf16[128,256]{1,0:T(8,128)(2,1)S(1)} %shard_map.112.refs_2_.r0), channel_id=1, source_target_pairs={{0,1},{1,2},{2,3},{3,0},{4,5},{5,6},{6,7},{7,4},{8,9},{9,10},{10,1... | collective-permute-start | bytes 196616 | tf_op jit(solution)/shard_map/ppermute | solution.py:344
  48.0 11.2 %collective-permute-start.6 = (bf16[128,256]{1,0:T(8,128)(2,1)S(1)}, bf16[128,256]{1,0:T(8,128)(2,1)S(1)}, u32[]{:S(2)}, u32[]{:S(2)}) collective-permute-start(bf16[128,256]{1,0:T(8,128)(2,1)S(1)} %shard_map.112.refs_2_.r0), channel_id=1, source_target_pairs={{0,3},{1,0},{2,1},{3,2},{4,7},{5,4},{6,5},{7,6},{8,11},{9,8},{10,9... | collective-permute-start | bytes 196616 | tf_op jit(solution)/shard_map/ppermute | solution.py:344
  49.5 9.7 %collective-permute-start.7 = (bf16[128,256]{1,0:T(8,128)(2,1)S(1)}, bf16[128,256]{1,0:T(8,128)(2,1)S(1)}, u32[]{:S(2)}, u32[]{:S(2)}) collective-permute-start(bf16[128,256]{1,0:T(8,128)(2,1)S(1)} %shard_map.112.refs_2_.r0), channel_id=1, source_target_pairs={{0,2},{1,3},{2,0},{3,1},{4,6},{5,7},{6,4},{7,5},{8,10},{9,11},{10,... | collective-permute-start | bytes 196616 | tf_op jit(solution)/shard_map/ppermute | solution.py:344
  50.9 10.5 %collective-permute-start.12 = (bf16[192,256]{1,0:T(8,128)(2,1)S(1)}, bf16[192,256]{1,0:T(8,128)(2,1)S(1)}, u32[]{:S(2)}, u32[]{:S(2)}) collective-permute-start(bf16[192,256]{1,0:T(8,128)(2,1)S(1)} %shard_map.111.after), channel_id=1, source_target_pairs={{2,0},{34,32},{67,65},{99,97},{128,130},{160,162},{193,195},{225,2... | collective-permute-start | bytes 294920 | tf_op jit(solution)/shard_map/ppermute | solution.py:340
  51.6 9.9 %collective-permute-start.13 = (bf16[192,256]{1,0:T(8,128)(2,1)S(1)}, bf16[192,256]{1,0:T(8,128)(2,1)S(1)}, u32[]{:S(2)}, u32[]{:S(2)}) collective-permute-start(bf16[192,256]{1,0:T(8,128)(2,1)S(1)} %shard_map.111.after), channel_id=1, source_target_pairs={{3,0},{35,32},{64,65},{96,97},{129,130},{161,162},{194,195},{226,2... | collective-permute-start | bytes 294920 | tf_op jit(solution)/shard_map/ppermute | solution.py:340
  58.5 3.0 %collective-permute-start.14 = (bf16[192,256]{1,0:T(8,128)(2,1)S(1)}, bf16[192,256]{1,0:T(8,128)(2,1)S(1)}, u32[]{:S(2)}, u32[]{:S(2)}) collective-permute-start(bf16[192,256]{1,0:T(8,128)(2,1)S(1)} %shard_map.111.after), channel_id=1, source_target_pairs={{1,0},{33,32},{66,65},{98,97},{131,130},{163,162},{192,195},{224,2... | collective-permute-start | bytes 294920 | tf_op jit(solution)/shard_map/ppermute | solution.py:340
  61.3 8.0 %collective-permute-start.10 = (bf16[64,2048]{1,0:T(8,128)(2,1)S(1)}, bf16[64,2048]{1,0:T(8,128)(2,1)S(1)}, u32[]{:S(2)}, u32[]{:S(2)}) collective-permute-start(bf16[64,2048]{1,0:T(8,128)(2,1)S(1)} %get-tuple-element.24), channel_id=1, source_target_pairs={{0,8},{4,28},{8,16},{12,4},{16,24},{20,12},{24,0},{28,20},{1,9},{5... | collective-permute-start | bytes 786440 | tf_op jit(solution)/shard_map/ppermute | solution.py:332
  61.6 16.3 %collective-permute-start.9 = (bf16[64,2048]{1,0:T(8,128)(2,1)S(1)}, bf16[64,2048]{1,0:T(8,128)(2,1)S(1)}, u32[]{:S(2)}, u32[]{:S(2)}) collective-permute-start(bf16[64,2048]{1,0:T(8,128)(2,1)S(1)} %get-tuple-element.22), channel_id=1, source_target_pairs={{0,24},{4,12},{8,0},{12,20},{16,8},{20,28},{24,16},{28,4},{1,25},{... | collective-permute-start | bytes 786440 | tf_op jit(solution)/shard_map/ppermute | solution.py:332
  69.4 8.5 %collective-permute-start.11 = (bf16[64,2048]{1,0:T(8,128)(2,1)S(1)}, bf16[64,2048]{1,0:T(8,128)(2,1)S(1)}, u32[]{:S(2)}, u32[]{:S(2)}) collective-permute-start(bf16[64,2048]{1,0:T(8,128)(2,1)S(1)} %add_convert_fusion), channel_id=1, source_target_pairs={{0,8},{4,28},{8,16},{12,4},{16,24},{20,12},{24,0},{28,20},{1,9},{5... | collective-permute-start | bytes 786440 | tf_op jit(solution)/shard_map/ppermute | solution.py:332
  69.5 4.9 %collective-permute-start.15 = (bf16[64,256]{1,0:T(8,128)(2,1)S(1)}, bf16[64,256]{1,0:T(8,128)(2,1)S(1)}, u32[]{:S(2)}, u32[]{:S(2)}) collective-permute-start(bf16[64,256]{1,0:T(8,128)(2,1)S(1)} %get-tuple-element.26), channel_id=1, source_target_pairs={{0,24},{4,12},{8,0},{12,20},{16,8},{20,28},{24,16},{28,4},{1,25},{... | collective-permute-start | bytes 98312 | tf_op jit(solution)/shard_map/ppermute | solution.py:332
  72.8 5.1 %collective-permute-start.16 = (bf16[64,256]{1,0:T(8,128)(2,1)S(1)}, bf16[64,256]{1,0:T(8,128)(2,1)S(1)}, u32[]{:S(2)}, u32[]{:S(2)}) collective-permute-start(bf16[64,256]{1,0:T(8,128)(2,1)S(1)} %get-tuple-element.25), channel_id=1, source_target_pairs={{0,8},{4,28},{8,16},{12,4},{16,24},{20,12},{24,0},{28,20},{1,9},{5... | collective-permute-start | bytes 98312 | tf_op jit(solution)/shard_map/ppermute | solution.py:332

commit v3 on v2

--- a/solution.py
+++ b/solution.py
@@ -242,24 +242,9 @@
     )(first, which, slots, *pieces, down_own, down_other, w_own, w_other, after)
 
 
-def expand_kernel(first, slots, r0, r1, r2, r3, up_own, up_other, o0, oa, ob, o2, spread):
-    outs = (o0, oa, ob, o2)
-    count = slots.shape[1]
+def scaled_rows(spread, up_own, up_other, outs):
     kept_rank, quarter = up_own.shape
-    piece = o0.shape[0]
-    rank = r0.shape[0] - piece
-    summed = (r0[...].astype(f32) + r1[...].astype(f32)) + (
-        r2[...].astype(f32) + r3[...].astype(f32)
-    )
-    ranks = summed[:rank, :].T
-    both = jnp.concatenate([ranks, ranks], axis=1)
-    slot_rows = jnp.broadcast_to(slots[...].astype(f32), (LANES, count)).T
-    part = lax.broadcasted_iota(jnp.int32, (1, LANES), 1) // rank
-    for which in range(2):
-        for j in range(kept_rank // LANES):
-            slot = (first[which] + 2 * j + part).astype(f32)
-            at = which * kept_rank + j * LANES
-            spread[:, at : at + LANES] = jnp.where(slot_rows == slot, both, 0.0).astype(bf16)
+    piece = outs[0].shape[0]
     step = 512
     for n in range(0, quarter, step):
         cols = slice(n, n + step)
@@ -270,53 +255,114 @@
         for k, o in enumerate(outs):
             o[:, cols] = delta[k * piece : (k + 1) * piece, :]
 
+
+def expand_last_kernel(first, slots, r0, r1, r2, r3, up_own, up_other, o2, spread, spread2):
+    count = slots.shape[1]
+    kept_rank = up_own.shape[0]
+    piece = o2.shape[0]
+    rank = r0.shape[0] - piece
+    head = count - piece
+    summed = (r0[...].astype(f32) + r1[...].astype(f32)) + (
+        r2[...].astype(f32) + r3[...].astype(f32)
+    )
+    ranks = summed[:rank, :].T
+    both = jnp.concatenate([ranks, ranks], axis=1)
+    slot_rows = jnp.broadcast_to(slots[...].astype(f32), (LANES, count)).T
+    part = lax.broadcasted_iota(jnp.int32, (1, LANES), 1) // rank
+    for which in range(2):
+        for j in range(kept_rank // LANES):
+            slot = (first[which] + 2 * j + part).astype(f32)
+            at = which * kept_rank + j * LANES
+            block = jnp.where(slot_rows == slot, both, 0.0).astype(bf16)
+            spread[:, at : at + LANES] = block[:head, :]
+            spread2[:, at : at + LANES] = block[head:, :]
+    scaled_rows(spread2, up_own, up_other, (o2,))
+
     @pl.when(first[3] == 1)
     def _():
         at = pl.ds(pl.multiple_of(first[2], LANES), count)
         o2[:, at] = (o2[:, at].astype(f32) + summed[rank:, :]).astype(bf16)
 
 
-def expand(first, slots, ranks, up_own, up_other):
+def expand_last(first, slots, ranks, up_own, up_other):
     count = slots.shape[1]
     kept_rank, quarter = up_own.shape
     piece = count // NY
     vmem = pl.BlockSpec(memory_space=pltpu.VMEM)
     smem = pl.BlockSpec(memory_space=pltpu.SMEM)
     return pl.pallas_call(
+        expand_last_kernel,
+        out_shape=(
+            jax.ShapeDtypeStruct((piece, quarter), bf16),
+            jax.ShapeDtypeStruct((count - piece, 2 * kept_rank), bf16),
+        ),
+        in_specs=[smem] + [vmem] * 7,
+        out_specs=(vmem,) * 2,
+        scratch_shapes=[pltpu.VMEM((piece, 2 * kept_rank), bf16)],
+        compiler_params=pltpu.CompilerParams(vmem_limit_bytes=10 * MIB),
+        cost_estimate=pl.CostEstimate(
+            flops=4 * piece * kept_rank * quarter, bytes_accessed=4 * MIB, transcendentals=0
+        ),
+    )(first, slots, *ranks, up_own, up_other)
+
+
+def expand_kernel(first, spread, up_own, up_other, base, *outs):
+    scaled_rows(spread, up_own, up_other, outs)
+
+    @pl.when(first[3] == 1)
+    def _():
+        piece = outs[0].shape[0]
+        at = pl.ds(pl.multiple_of(first[2], LANES), base.shape[1])
+        for k, o in enumerate(outs):
+            o[:, at] = (o[:, at].astype(f32) + base[k * piece : (k + 1) * piece, :]).astype(bf16)
+
+
+def expand(first, spread, up_own, up_other, base):
+    quarter = up_own.shape[1]
+    piece = spread.shape[0] // (NY - 1)
+    vmem = pl.BlockSpec(memory_space=pltpu.VMEM)
+    return pl.pallas_call(
         expand_kernel,
-        out_shape=(jax.ShapeDtypeStruct((piece, quarter), bf16),) * 4,
-        in_specs=[smem] + [vmem] * 7,
-        out_specs=(vmem,) * 4,
-        scratch_shapes=[pltpu.VMEM((count, 2 * kept_rank), bf16)],
-        compiler_params=pltpu.CompilerParams(vmem_limit_bytes=12 * MIB),
+        out_shape=(jax.ShapeDtypeStruct((piece, quarter), bf16),) * (NY - 1),
+        in_specs=[pl.BlockSpec(memory_space=pltpu.SMEM)] + [vmem] * 4,
+        out_specs=(vmem,) * (NY - 1),
+        compiler_params=pltpu.CompilerParams(vmem_limit_bytes=10 * MIB),
         cost_estimate=pl.CostEstimate(
-            flops=4 * count * kept_rank * quarter, bytes_accessed=6 * MIB, transcendentals=0
-        ),
-    )(first, slots, *ranks, up_own, up_other)
-
-
-def join_kernel(place, d0, ea, eb, b0, b1, b2, out):
-    out[...] = ((d0[...].astype(f32) + ea[...].astype(f32)) + eb[...].astype(f32)).astype(bf16)
-
-    @pl.when(place[3] == 1)
-    def _():
-        cols = b0.shape[1]
-        for i, b in enumerate((b0, b1, b2)):
-            at = pl.ds(pl.multiple_of(place[i], LANES), cols)
-            total = (d0[:, at].astype(f32) + ea[:, at].astype(f32)) + eb[:, at].astype(f32)
-            out[:, at] = (total + b[...].astype(f32)).astype(bf16)
-
-
-def join(place, rows, bases):
-    vmem = pl.BlockSpec(memory_space=pltpu.VMEM)
-    return pl.pallas_call(
-        join_kernel,
-        out_shape=jax.ShapeDtypeStruct(rows[0].shape, bf16),
-        in_specs=[pl.BlockSpec(memory_space=pltpu.SMEM)] + [vmem] * 6,
-        out_specs=vmem,
-        compiler_params=pltpu.CompilerParams(vmem_limit_bytes=8 * MIB),
-        cost_estimate=pl.CostEstimate(flops=MIB, bytes_accessed=MIB, transcendentals=0),
-    )(place, *rows, *bases)
+            flops=2 * spread.size * quarter, bytes_accessed=5 * MIB, transcendentals=0
+        ),
+    )(first, spread, up_own, up_other, base)
+
+
+def gather_kernel(up_own, up_other, b0, b1, b2, b3, after, own_out, other_out, base_out, sems):
+    copies = [
+        pltpu.make_async_copy(src, dst, sems.at[i])
+        for i, (src, dst) in enumerate(((up_own, own_out), (up_other, other_out)))
+    ]
+    for copy in copies:
+        copy.start()
+    base_out[...] = (b0[...].astype(f32) + b1[...].astype(f32)) + (
+        b2[...].astype(f32) + b3[...].astype(f32)
+    )
+    for copy in copies:
+        copy.wait()
+
+
+def gather_ups(up_own, up_other, parts, after):
+    vmem = pl.BlockSpec(memory_space=pltpu.VMEM)
+    anywhere = pl.BlockSpec(memory_space=pl.ANY)
+    return pl.pallas_call(
+        gather_kernel,
+        out_shape=(
+            jax.ShapeDtypeStruct(up_own.shape, bf16),
+            jax.ShapeDtypeStruct(up_other.shape, bf16),
+            jax.ShapeDtypeStruct(parts[0].shape, f32),
+        ),
+        in_specs=[anywhere] * 2 + [vmem] * NX + [anywhere],
+        out_specs=(vmem,) * 3,
+        scratch_shapes=[pltpu.SemaphoreType.DMA((2,))],
+        compiler_params=pltpu.CompilerParams(vmem_limit_bytes=10 * MIB),
+        cost_estimate=pl.CostEstimate(flops=MIB, bytes_accessed=8 * MIB, transcendentals=0),
+    )(*in_hbm(up_own, up_other), *parts, after)
 
 
 def swap_cores(x):
@@ -377,15 +423,10 @@
         position,
         NZ,
     )
-    copies, down, up, output_weight = lax.optimization_barrier((copies, down, up, output_weight))
     down_other = swap_cores(down)
     w_other = swap_cores(output_weight)
     up_other = swap_cores(up)
     p0 = lax.all_to_all(copies, "z", 0, 0, tiled=True).reshape(block, features)
-
-    pa = along_y(p0, 1)
-    pb = along_y(p0, -1)
-    p2 = along_y(pa, 1)
 
     tenants_all = tenant_adapter_index.shape[0]
     matches = tenant[:, None] == jnp.arange(tenants_all, dtype=jnp.int32)[None, :]
@@ -396,6 +437,10 @@
     pick = (ys + core * NY)[:, None] == jnp.arange(NC * NY, dtype=jnp.int32)[None, :]
     slots = jnp.sum(jnp.where(pick[:, :, None], table[None], 0), axis=1).reshape(1, NY * block)
 
+    pa = along_y(p0, 1)
+    pb = along_y(p0, -1)
+    p2 = along_y(pa, 1)
+
     add = lambda *xs: functools.reduce(jnp.add, [x.astype(f32) for x in xs]).astype(bf16)
     is_root = (x_here == z_here // (NZ // NX)).astype(jnp.int32)
     width = NC * cols
@@ -405,23 +450,19 @@
 
     (down_other,) = stage((down_other,), p0)
     base_part = base_terms(which, (p0, pa, pb), output_weight, w_other)
-    sums = [base_part] + [to_root(base_part, s) for s in (2, 1, 3)]
     packed = rank_terms(
         first, which, slots, (p0, pa, pb, p2), down, down_other, output_weight, w_other, base_part
     )
     packs = [packed] + [along_x(packed, s) for s in (1, 3, 2)]
-    base = add(*sums).reshape(NY - 1, block, width)
-    bases = [base[0], along_y(base[1], -1), along_y(base[2], 1)]
-    senders = jnp.stack([y_here, y_here + ahead, y_here - ahead]) % NY
-    place = jnp.concatenate([(columns + senders) * width, is_root[None]])
-
-    ups = stage((up, up_other), packed)
-    d0, da, db, d2 = expand(first, slots, packs, *ups)
-
+    sums = [base_part] + [to_root(base_part, s) for s in (2, 1, 3)]
+    *ups, base = gather_ups(up, up_other, sums, packed)
+    d2, spread = expand_last(first, slots, packs, *ups)
     e2 = along_y(d2, 1)
+    d0, da, db = expand(first, spread, *ups, base)
+
     ea = along_y(da, -1)
     eb = along_y(add(db, e2), 1)
-    home_rows = join(place, (d0, ea, eb), bases)
+    home_rows = add(d0, ea, eb)
     got = lax.all_to_all(home_rows.reshape(NZ, mine_n, quarter), "z", 0, 0, tiled=True)
     return jnp.sum(got.astype(f32), axis=0).astype(bf16)
 

time: 93.1 us -> 89.3 us (0.959)
  starting transfers between devices: 29.3 us -> 25.8 us
  blocking collectives: 12.9 us -> 14.7 us
  waiting for transfers between devices: 31.1 us -> 30.1 us
    pallas_call x1 -> x2, Pallas kernels: 0.64 us -> 3.86 us  [the longest x1 2.24 us: gather_ups(): pl.pallas_call(gather_kernel, out_shape=(jax.ShapeDtypeStruct(up_own.shap...]
    ppermute x8 -> x6, waiting for transfers between devices: 19.3 us -> 16.8 us  [along_y(): return lax.ppermute(x, ('y', 'c'), pairs)]
    pallas_call x2 -> x1, Pallas kernels: 3.84 us -> 1.6 us  [stage(): pl.pallas_call(stage_kernel, out_shape=tuple((jax.ShapeDtypeStruct(x.shap...]
    ppermute x8 -> x6, starting transfers between devices: 10.7 us -> 8.54 us  [along_y(): return lax.ppermute(x, ('y', 'c'), pairs)]
    ppermute x3, starting transfers between devices: 5.95 us -> 3.85 us  [to_root(): return lax.ppermute(x, ('z', 'x'), pairs)]
    all_to_all x1, blocking collectives: 12.9 us -> 14.7 us  [local(): lax.all_to_all(home_rows.reshape(NZ, mine_n, quarter), 'z', 0, 0, tiled=T...]
    ppermute x3, waiting for transfers between devices: 0.01 us -> 1.44 us  [along_x(): return lax.ppermute(x, 'x', [(i, (i + shift) % NX) for i in range(NX)])]
  transfers between devices with their start and end apart: 18 -> 16, of which waited for: 6 -> 6; matrix products, arithmetic and copies ran while one was open for 1% -> 1% of each run, Pallas kernels for 11% -> 16%
where the time goes in v3:
time: 89.3 us; the launch traced here: 88.4 us
  waiting for transfers between devices  30.1 us (34%)
  starting transfers between devices  25.8 us (29%)
  Pallas kernels  15.9 us (18%)
  blocking collectives  14.7 us (16%)
  other arithmetic  1.47 us (2%)
    ppermute x6, waiting for transfers between devices, along_y(): return lax.ppermute(x, ('y', 'c'), pairs)  16.8 us
    all_to_all x1, blocking collectives, local(): lax.all_to_all(home_rows.reshape(NZ, mine_n, quarter), 'z', 0, 0, tiled=T...  14.7 us
    all_to_all x1, waiting for transfers between devices, local(): p0 = lax.all_to_all(copies, 'z', 0, 0, tiled=True).reshape(block, features)  11.8 us
    ppermute x6, starting transfers between devices, along_y(): return lax.ppermute(x, ('y', 'c'), pairs)  8.54 us
    all_to_all x1, starting transfers between devices, local(): p0 = lax.all_to_all(copies, 'z', 0, 0, tiled=True).reshape(block, features)  8.48 us
    pallas_call x1, Pallas kernels, attend(): pl.pallas_call(attend_kernel, out_shape=jax.ShapeDtypeStruct((repeats, se...  5.77 us
    ppermute x3, starting transfers between devices, along_x(): return lax.ppermute(x, 'x', [(i, (i + shift) % NX) for i in range(NX)])  4.35 us
    ppermute x3, starting transfers between devices, to_root(): return lax.ppermute(x, ('z', 'x'), pairs)  3.85 us
  transfers between devices with their start and end apart: 16, of which 6 were waited for; matrix products, arithmetic and copies ran while one was open for 1% of the time, Pallas kernels for 16%

profile of v3, /device:TPU:6, one launch (start us, length us, event | category | flops | bytes accessed | tf_op | source)
XLA Modules:
  0.0 88.4 jit_solution(11671356677654211342)
XLA Ops:
  0.0 0.0 collective-permute-start.3
  0.0 0.5 collective-permute-start.8
  0.5 5.8 %shard_map.109 = bf16[8,8,2048]{2,1,0:T(8,128)(2,1)} custom-call(s32[8]{0:T(128)} %position.1, bf16[8,2048]{1,0:T(8,128)(2,1)} %query.1, bf16[8,256]{1,0:T(8,128)(2,1)} %fresh_key.1, bf16[8,256]{1,0:T(8,128)(2,1)} %fresh_value.1, bf16[8,1024,256]{2,1,0:T(8,128)(2,1)} %keys.1, bf16[8,1024,256]{2,1,0:T(8,128)(2,1)} %values.1), custom_call_target="tpu_custom_call" | custom-call | flops 134217728 | bytes 8388608 | tf_op jit(solution)/shard_map/pallas_call | solution.py:120
  6.3 8.5 %all-to-all-start = ((bf16[8,8,2048]{2,1,0:T(8,128)(2,1)}), bf16[8,8,2048]{2,1,0:T(8,128)(2,1)S(1)}, u32[]{:S(2)}, u32[]{:S(2)}) async-start(bf16[8,8,2048]{2,1,0:T(8,128)(2,1)} %shard_map.109), calls=%async_computation | async-start | bytes 524288 | tf_op jit(solution)/shard_map/all_to_all | solution.py:429
  14.8 0.1 collective-permute-start.4
  14.9 0.2 select_reduce_fusion
  15.2 11.8 %all-to-all-done = bf16[8,8,2048]{2,1,0:T(8,128)(2,1)S(1)} async-done(((bf16[8,8,2048]{2,1,0:T(8,128)(2,1)}), bf16[8,8,2048]{2,1,0:T(8,128)(2,1)S(1)}, u32[]{:S(2)}, u32[]{:S(2)}) %all-to-all-start) | async-done | bytes 262176 | tf_op jit(solution)/shard_map/all_to_all | solution.py:429
  27.0 1.6 %collective-permute-start = (bf16[64,2048]{1,0:T(8,128)(2,1)S(1)}, bf16[64,2048]{1,0:T(8,128)(2,1)S(1)}, u32[]{:S(2)}, u32[]{:S(2)}) collective-permute-start(bf16[64,2048]{1,0:T(8,128)(2,1)S(1)} %bitcast.18), channel_id=1, source_target_pairs={{0,8},{4,28},{8,16},{12,4},{16,24},{20,12},{24,0},{28,20},{1,9},{5... | collective-permute-start | bytes 786440 | tf_op jit(solution)/shard_map/ppermute | solution.py:378
  28.6 0.1 fusion.1
  28.6 0.1 reshape.130
  28.8 0.1 broadcast_in_dim.43
  28.9 0.1 iota_compare_fusion.1
  28.9 1.7 %collective-permute-start.1 = (bf16[64,2048]{1,0:T(8,128)(2,1)S(1)}, bf16[64,2048]{1,0:T(8,128)(2,1)S(1)}, u32[]{:S(2)}, u32[]{:S(2)}) collective-permute-start(bf16[64,2048]{1,0:T(8,128)(2,1)S(1)} %bitcast.19), channel_id=1, source_target_pairs={{0,24},{4,12},{8,0},{12,20},{16,8},{20,28},{24,16},{28,4},{1,25},{... | collective-permute-start | bytes 786440 | tf_op jit(solution)/shard_map/ppermute | solution.py:378
  30.6 5.8 %collective-permute-done.pa = bf16[64,2048]{1,0:T(8,128)(2,1)S(1)} collective-permute-done((bf16[64,2048]{1,0:T(8,128)(2,1)S(1)}, bf16[64,2048]{1,0:T(8,128)(2,1)S(1)}, u32[]{:S(2)}, u32[]{:S(2)}) %collective-permute-start) | collective-permute-done | bytes 262176 | tf_op jit(solution)/shard_map/ppermute | solution.py:378
  36.3 1.1 %collective-permute-start.2 = (bf16[64,2048]{1,0:T(8,128)(2,1)S(1)}, bf16[64,2048]{1,0:T(8,128)(2,1)S(1)}, u32[]{:S(2)}, u32[]{:S(2)}) collective-permute-start(bf16[64,2048]{1,0:T(8,128)(2,1)S(1)} %collective-permute-done.pa), channel_id=1, source_target_pairs={{0,8},{4,28},{8,16},{12,4},{16,24},{20,12},{24,0},{28,20},{1,9},{5... | collective-permute-start | bytes 786440 | tf_op jit(solution)/shard_map/ppermute | solution.py:378
  37.5 0.1 select_reduce_fusion.1
  37.6 0.1 reshape.131.slots
  37.7 0.1 pad_add_fusion.1.which
  37.7 0.1 pad_add_fusion.first
  37.8 0.0 collective-permute-done.4.w_other
  37.8 0.0 collective-permute-done.1.pb
  37.8 1.1 %shard_map.111.after.b0 = bf16[192,256]{1,0:T(8,128)(2,1)S(1)} custom-call(s32[2]{0:T(128)S(1)} %pad_add_fusion.1.which, bf16[64,2048]{1,0:T(8,128)(2,1)S(1)} %bitcast.20, bf16[64,2048]{1,0:T(8,128)(2,1)S(1)} %collective-permute-done.pa, bf16[64,2048]{1,0:T(8,128)(2,1)S(1)} %collective-permute-done.1.pb, bf16[2048,128]{1,0:T(8,128)(2,1)S(1)} %copy-done.1, ...), custom_call_target="tpu_custom_call" | custom-call | flops 201326592 | bytes 2097152 | tf_op jit(solution)/shard_map/pallas_call | solution.py:188
  38.9 0.0 copy-start
  39.0 2.5 %collective-permute-start.10 = (bf16[192,256]{1,0:T(8,128)(2,1)S(1)}, bf16[192,256]{1,0:T(8,128)(2,1)S(1)}, u32[]{:S(2)}, u32[]{:S(2)}) collective-permute-start(bf16[192,256]{1,0:T(8,128)(2,1)S(1)} %shard_map.111.after.b0), channel_id=1, source_target_pairs={{3,0},{35,32},{64,65},{96,97},{129,130},{161,162},{194,195},{226,2... | collective-permute-start | bytes 294920 | tf_op jit(solution)/shard_map/ppermute | solution.py:386
  41.5 0.7 collective-permute-start.11
  42.2 0.7 collective-permute-start.9
  42.8 1.6 %shard_map.110.down_other = bf16[8,64,2048]{2,1,0:T(8,128)(2,1)S(1)} custom-call(bf16[8,64,2048]{2,1,0:T(8,128)(2,1)} %collective-permute-done.3.refs_0_, bf16[64,2048]{1,0:T(8,128)(2,1)S(1)} %bitcast.21), custom_call_target="tpu_custom_call" | custom-call | bytes 8388608 | tf_op jit(solution)/shard_map/pallas_call | solution.py:164
  44.4 0.0 collective-permute-done.2.p2
  44.5 2.0 %shard_map.112.after.r0 = bf16[128,256]{1,0:T(8,128)(2,1)S(1)} custom-call(s32[4]{0:T(128)S(1)} %pad_add_fusion.first, s32[2]{0:T(128)S(1)} %pad_add_fusion.1.which, s32[1,256]{1,0:T(1,128)S(1)} %reshape.131.slots, bf16[64,2048]{1,0:T(8,128)(2,1)S(1)} %bitcast.22, bf16[64,2048]{1,0:T(8,128)(2,1)S(1)} %collective-permute-done.pa, ...), custom_call_target="tpu_custom_call" | custom-call | flops 1073741824 | bytes 6291456 | tf_op jit(solution)/shard_map/pallas_call | solution.py:232
  46.5 0.7 collective-permute-start.5
  47.2 1.6 %collective-permute-start.6 = (bf16[128,256]{1,0:T(8,128)(2,1)S(1)}, bf16[128,256]{1,0:T(8,128)(2,1)S(1)}, u32[]{:S(2)}, u32[]{:S(2)}) collective-permute-start(bf16[128,256]{1,0:T(8,128)(2,1)S(1)} %shard_map.112.after.r0), channel_id=1, source_target_pairs={{0,3},{1,0},{2,1},{3,2},{4,7},{5,4},{6,5},{7,6},{8,11},{9,8},{10,9... | collective-permute-start | bytes 196616 | tf_op jit(solution)/shard_map/ppermute | solution.py:390
  48.7 0.0 collective-permute-done.11.b3
  48.8 2.1 %collective-permute-start.7 = (bf16[128,256]{1,0:T(8,128)(2,1)S(1)}, bf16[128,256]{1,0:T(8,128)(2,1)S(1)}, u32[]{:S(2)}, u32[]{:S(2)}) collective-permute-start(bf16[128,256]{1,0:T(8,128)(2,1)S(1)} %shard_map.112.after.r0), channel_id=1, source_target_pairs={{0,2},{1,3},{2,0},{3,1},{4,6},{5,7},{6,4},{7,5},{8,10},{9,11},{10,... | collective-permute-start | bytes 196616 | tf_op jit(solution)/shard_map/ppermute | solution.py:390
  50.8 2.2 %shard_map.113 = (bf16[512,2048]{1,0:T(8,128)(2,1)S(1)}, bf16[512,2048]{1,0:T(8,128)(2,1)S(1)}, f32[192,256]{1,0:T(8,128)S(1)}) custom-call(bf16[512,2048]{1,0:T(8,128)(2,1)} %bitcast.26, bf16[512,2048]{1,0:T(8,128)(2,1)} %collective-permute-done.8.up_other, bf16[192,256]{1,0:T(8,128)(2,1)S(1)} %shard_map.111.after.b0, ...), custom_call_target="tpu_custom_call" | custom-call | flops 1048576 | bytes 8388608 | tf_op jit(solution)/shard_map/pallas_call | solution.py:353
  53.1 0.0 collective-permute-done.6.r2
  53.1 1.4 %collective-permute-done.7.r3 = bf16[128,256]{1,0:T(8,128)(2,1)S(1)} collective-permute-done((bf16[128,256]{1,0:T(8,128)(2,1)S(1)}, bf16[128,256]{1,0:T(8,128)(2,1)S(1)}, u32[]{:S(2)}, u32[]{:S(2)}) %collective-permute-start.7) | collective-permute-done | bytes 65568 | tf_op jit(solution)/shard_map/ppermute | solution.py:390
  54.5 1.6 %shard_map.114 = (bf16[64,2048]{1,0:T(8,128)(2,1)S(1)}, bf16[192,1024]{1,0:T(8,128)(2,1)S(1)}) custom-call(s32[4]{0:T(128)S(1)} %pad_add_fusion.first, s32[1,256]{1,0:T(1,128)S(1)} %reshape.131.slots, bf16[128,256]{1,0:T(8,128)(2,1)S(1)} %shard_map.112.after.r0, bf16[128,256]{1,0:T(8,128)(2,1)S(1)} %collective-permute-done.5.r1, ...), custom_call_target="tpu_custom_call" | custom-call | flops 268435456 | bytes 4194304 | tf_op jit(solution)/shard_map/pallas_call | solution.py:293
  56.1 0.6 collective-permute-start.13
  56.7 1.6 %shard_map.115 = (bf16[64,2048]{1,0:T(8,128)(2,1)S(1)}, bf16[64,2048]{1,0:T(8,128)(2,1)S(1)}, bf16[64,2048]{1,0:T(8,128)(2,1)S(1)}) custom-call(s32[4]{0:T(128)S(1)} %pad_add_fusion.first, bf16[192,1024]{1,0:T(8,128)(2,1)S(1)} %get-tuple-element.15.spread, bf16[512,2048]{1,0:T(8,128)(2,1)S(1)} %get-tuple-element.13.up_own, ...), custom_call_target="tpu_custom_call" | custom-call | flops 805306368 | bytes 5242880 | tf_op jit(solution)/shard_map/pallas_call | solution.py:324
  58.3 3.0 %collective-permute-start.12 = (bf16[64,2048]{1,0:T(8,128)(2,1)S(1)}, bf16[64,2048]{1,0:T(8,128)(2,1)S(1)}, u32[]{:S(2)}, u32[]{:S(2)}) collective-permute-start(bf16[64,2048]{1,0:T(8,128)(2,1)S(1)} %get-tuple-element.18), channel_id=1, source_target_pairs={{0,24},{4,12},{8,0},{12,20},{16,8},{20,28},{24,16},{28,4},{1,25},{... | collective-permute-start | bytes 786440 | tf_op jit(solution)/shard_map/ppermute | solution.py:378
  61.3 4.0 %collective-permute-done.13 = bf16[64,2048]{1,0:T(8,128)(2,1)S(1)} collective-permute-done((bf16[64,2048]{1,0:T(8,128)(2,1)S(1)}, bf16[64,2048]{1,0:T(8,128)(2,1)S(1)}, u32[]{:S(2)}, u32[]{:S(2)}) %collective-permute-start.13) | collective-permute-done | bytes 262176 | tf_op jit(solution)/shard_map/ppermute | solution.py:378
  65.3 0.1 add_convert_fusion.1
  65.4 0.6 collective-permute-start.14
  66.0 1.4 %collective-permute-done.12 = bf16[64,2048]{1,0:T(8,128)(2,1)S(1)} collective-permute-done((bf16[64,2048]{1,0:T(8,128)(2,1)S(1)}, bf16[64,2048]{1,0:T(8,128)(2,1)S(1)}, u32[]{:S(2)}, u32[]{:S(2)}) %collective-permute-start.12) | collective-permute-done | bytes 262176 | tf_op jit(solution)/shard_map/ppermute | solution.py:378
  67.3 5.7 %collective-permute-done.14 = bf16[64,2048]{1,0:T(8,128)(2,1)S(1)} collective-permute-done((bf16[64,2048]{1,0:T(8,128)(2,1)S(1)}, bf16[64,2048]{1,0:T(8,128)(2,1)S(1)}, u32[]{:S(2)}, u32[]{:S(2)}) %collective-permute-start.14) | collective-permute-done | bytes 262176 | tf_op jit(solution)/shard_map/ppermute | solution.py:378
  73.0 0.1 fusion
  73.1 14.7 %all_to_all.10 = bf16[8,8,2048]{2,1,0:T(8,128)(2,1)S(1)} all-to-all(bf16[8,8,2048]{2,1,0:T(8,128)(2,1)S(1)} %fusion), channel_id=1, replica_groups=mesh['z'=8,'y'=4,'c'=2,'x'=4] {'z'}, dimensions={0} | all-to-all | bytes 524288 | tf_op jit(solution)/shard_map/all_to_all | solution.py:466
  87.8 0.7 reduce_sum.32
  (13 shorter events, 0.0 us)
Async XLA Ops:
  0.0 42.2 %collective-permute-start.3 = (bf16[8,64,2048]{2,1,0:T(8,128)(2,1)}, bf16[8,64,2048]{2,1,0:T(8,128)(2,1)}, u32[]{:S(2)}, u32[]{:S(2)}) collective-permute-start(bf16[8,64,2048]{2,1,0:T(8,128)(2,1)} %bitcast.23), channel_id=1, source_target_pairs={{0,4},{4,0},{1,5},{5,1},{2,6},{6,2},{3,7},{7,3},{8,12},{12,8},{9,1... | collective-permute-start | bytes 6291464 | tf_op jit(solution)/shard_map/ppermute | solution.py:369
  0.0 14.8 %copy-start.1 = (bf16[2048,128]{1,0:T(8,128)(2,1)S(1)}, bf16[2048,128]{1,0:T(8,128)(2,1)}, u32[]{:S(2)}) copy-start(bf16[2048,128]{1,0:T(8,128)(2,1)} %w_own.3) | copy-start | bytes 1572868
  0.0 14.9 %copy-start.2 = (s32[512]{0:T(512)S(1)}, s32[512]{0:T(512)}, u32[]{:S(2)}) copy-start(s32[512]{0:T(512)} %param.18) | copy-start | bytes 6148
  0.0 14.9 %copy-start.3 = (s32[512]{0:T(512)S(1)}, s32[512]{0:T(512)}, u32[]{:S(2)}) copy-start(s32[512]{0:T(512)} %param.17) | copy-start | bytes 6148
  0.0 50.8 %collective-permute-start.8 = (bf16[512,2048]{1,0:T(8,128)(2,1)}, bf16[512,2048]{1,0:T(8,128)(2,1)}, u32[]{:S(2)}, u32[]{:S(2)}) collective-permute-start(bf16[512,2048]{1,0:T(8,128)(2,1)} %bitcast.25), channel_id=1, source_target_pairs={{0,4},{4,0},{1,5},{5,1},{2,6},{6,2},{3,7},{7,3},{8,12},{12,8},{9,1... | collective-permute-start | bytes 6291464 | tf_op jit(solution)/shard_map/ppermute | solution.py:369
  6.3 20.7 %all-to-all-start = ((bf16[8,8,2048]{2,1,0:T(8,128)(2,1)}), bf16[8,8,2048]{2,1,0:T(8,128)(2,1)S(1)}, u32[]{:S(2)}, u32[]{:S(2)}) async-start(bf16[8,8,2048]{2,1,0:T(8,128)(2,1)} %shard_map.109), calls=%async_computation | async-start | bytes 524288 | tf_op jit(solution)/shard_map/all_to_all | solution.py:429
  14.8 23.1 %collective-permute-start.4 = (bf16[2048,128]{1,0:T(8,128)(2,1)S(1)}, bf16[2048,128]{1,0:T(8,128)(2,1)S(1)}, u32[]{:S(2)}, u32[]{:S(2)}) collective-permute-start(bf16[2048,128]{1,0:T(8,128)(2,1)S(1)} %copy-done.1), channel_id=1, source_target_pairs={{0,4},{4,0},{1,5},{5,1},{2,6},{6,2},{3,7},{7,3},{8,12},{12,8},{9,1... | collective-permute-start | bytes 1572872 | tf_op jit(solution)/shard_map/ppermute | solution.py:369
  27.0 9.4 %collective-permute-start = (bf16[64,2048]{1,0:T(8,128)(2,1)S(1)}, bf16[64,2048]{1,0:T(8,128)(2,1)S(1)}, u32[]{:S(2)}, u32[]{:S(2)}) collective-permute-start(bf16[64,2048]{1,0:T(8,128)(2,1)S(1)} %bitcast.18), channel_id=1, source_target_pairs={{0,8},{4,28},{8,16},{12,4},{16,24},{20,12},{24,0},{28,20},{1,9},{5... | collective-permute-start | bytes 786440 | tf_op jit(solution)/shard_map/ppermute | solution.py:378
  28.9 8.9 %collective-permute-start.1 = (bf16[64,2048]{1,0:T(8,128)(2,1)S(1)}, bf16[64,2048]{1,0:T(8,128)(2,1)S(1)}, u32[]{:S(2)}, u32[]{:S(2)}) collective-permute-start(bf16[64,2048]{1,0:T(8,128)(2,1)S(1)} %bitcast.19), channel_id=1, source_target_pairs={{0,24},{4,12},{8,0},{12,20},{16,8},{20,28},{24,16},{28,4},{1,25},{... | collective-permute-start | bytes 786440 | tf_op jit(solution)/shard_map/ppermute | solution.py:378
  36.3 8.1 %collective-permute-start.2 = (bf16[64,2048]{1,0:T(8,128)(2,1)S(1)}, bf16[64,2048]{1,0:T(8,128)(2,1)S(1)}, u32[]{:S(2)}, u32[]{:S(2)}) collective-permute-start(bf16[64,2048]{1,0:T(8,128)(2,1)S(1)} %collective-permute-done.pa), channel_id=1, source_target_pairs={{0,8},{4,28},{8,16},{12,4},{16,24},{20,12},{24,0},{28,20},{1,9},{5... | collective-permute-start | bytes 786440 | tf_op jit(solution)/shard_map/ppermute | solution.py:378
  38.9 5.5 %copy-start = (bf16[8,2048,64]{1,2,0:T(8,128)(2,1)S(1)}, bf16[8,2048,64]{1,2,0:T(8,128)(2,1)}, u32[]{:S(2)}) copy-start(bf16[8,2048,64]{1,2,0:T(8,128)(2,1)} %param.20) | copy-start | bytes 6291460
  39.0 8.2 %collective-permute-start.10 = (bf16[192,256]{1,0:T(8,128)(2,1)S(1)}, bf16[192,256]{1,0:T(8,128)(2,1)S(1)}, u32[]{:S(2)}, u32[]{:S(2)}) collective-permute-start(bf16[192,256]{1,0:T(8,128)(2,1)S(1)} %shard_map.111.after.b0), channel_id=1, source_target_pairs={{3,0},{35,32},{64,65},{96,97},{129,130},{161,162},{194,195},{226,2... | collective-permute-start | bytes 294920 | tf_op jit(solution)/shard_map/ppermute | solution.py:386
  41.5 7.3 %collective-permute-start.11 = (bf16[192,256]{1,0:T(8,128)(2,1)S(1)}, bf16[192,256]{1,0:T(8,128)(2,1)S(1)}, u32[]{:S(2)}, u32[]{:S(2)}) collective-permute-start(bf16[192,256]{1,0:T(8,128)(2,1)S(1)} %shard_map.111.after.b0), channel_id=1, source_target_pairs={{1,0},{33,32},{66,65},{98,97},{131,130},{163,162},{192,195},{224,2... | collective-permute-start | bytes 294920 | tf_op jit(solution)/shard_map/ppermute | solution.py:386
  42.2 8.7 %collective-permute-start.9 = (bf16[192,256]{1,0:T(8,128)(2,1)S(1)}, bf16[192,256]{1,0:T(8,128)(2,1)S(1)}, u32[]{:S(2)}, u32[]{:S(2)}) collective-permute-start(bf16[192,256]{1,0:T(8,128)(2,1)S(1)} %shard_map.111.after.b0), channel_id=1, source_target_pairs={{2,0},{34,32},{67,65},{99,97},{128,130},{160,162},{193,195},{225,2... | collective-permute-start | bytes 294920 | tf_op jit(solution)/shard_map/ppermute | solution.py:386
  46.5 6.6 %collective-permute-start.5 = (bf16[128,256]{1,0:T(8,128)(2,1)S(1)}, bf16[128,256]{1,0:T(8,128)(2,1)S(1)}, u32[]{:S(2)}, u32[]{:S(2)}) collective-permute-start(bf16[128,256]{1,0:T(8,128)(2,1)S(1)} %shard_map.112.after.r0), channel_id=1, source_target_pairs={{0,1},{1,2},{2,3},{3,0},{4,5},{5,6},{6,7},{7,4},{8,9},{9,10},{10,1... | collective-permute-start | bytes 196616 | tf_op jit(solution)/shard_map/ppermute | solution.py:390
  47.2 5.9 %collective-permute-start.6 = (bf16[128,256]{1,0:T(8,128)(2,1)S(1)}, bf16[128,256]{1,0:T(8,128)(2,1)S(1)}, u32[]{:S(2)}, u32[]{:S(2)}) collective-permute-start(bf16[128,256]{1,0:T(8,128)(2,1)S(1)} %shard_map.112.after.r0), channel_id=1, source_target_pairs={{0,3},{1,0},{2,1},{3,2},{4,7},{5,4},{6,5},{7,6},{8,11},{9,8},{10,9... | collective-permute-start | bytes 196616 | tf_op jit(solution)/shard_map/ppermute | solution.py:390
  48.8 5.8 %collective-permute-start.7 = (bf16[128,256]{1,0:T(8,128)(2,1)S(1)}, bf16[128,256]{1,0:T(8,128)(2,1)S(1)}, u32[]{:S(2)}, u32[]{:S(2)}) collective-permute-start(bf16[128,256]{1,0:T(8,128)(2,1)S(1)} %shard_map.112.after.r0), channel_id=1, source_target_pairs={{0,2},{1,3},{2,0},{3,1},{4,6},{5,7},{6,4},{7,5},{8,10},{9,11},{10,... | collective-permute-start | bytes 196616 | tf_op jit(solution)/shard_map/ppermute | solution.py:390
  56.1 9.1 %collective-permute-start.13 = (bf16[64,2048]{1,0:T(8,128)(2,1)S(1)}, bf16[64,2048]{1,0:T(8,128)(2,1)S(1)}, u32[]{:S(2)}, u32[]{:S(2)}) collective-permute-start(bf16[64,2048]{1,0:T(8,128)(2,1)S(1)} %get-tuple-element.20), channel_id=1, source_target_pairs={{0,8},{4,28},{8,16},{12,4},{16,24},{20,12},{24,0},{28,20},{1,9},{5... | collective-permute-start | bytes 786440 | tf_op jit(solution)/shard_map/ppermute | solution.py:378
  58.3 9.0 %collective-permute-start.12 = (bf16[64,2048]{1,0:T(8,128)(2,1)S(1)}, bf16[64,2048]{1,0:T(8,128)(2,1)S(1)}, u32[]{:S(2)}, u32[]{:S(2)}) collective-permute-start(bf16[64,2048]{1,0:T(8,128)(2,1)S(1)} %get-tuple-element.18), channel_id=1, source_target_pairs={{0,24},{4,12},{8,0},{12,20},{16,8},{20,28},{24,16},{28,4},{1,25},{... | collective-permute-start | bytes 786440 | tf_op jit(solution)/shard_map/ppermute | solution.py:378
  65.4 7.7 %collective-permute-start.14 = (bf16[64,2048]{1,0:T(8,128)(2,1)S(1)}, bf16[64,2048]{1,0:T(8,128)(2,1)S(1)}, u32[]{:S(2)}, u32[]{:S(2)}) collective-permute-start(bf16[64,2048]{1,0:T(8,128)(2,1)S(1)} %add_convert_fusion.1), channel_id=1, source_target_pairs={{0,8},{4,28},{8,16},{12,4},{16,24},{20,12},{24,0},{28,20},{1,9},{5... | collective-permute-start | bytes 786440 | tf_op jit(solution)/shard_map/ppermute | solution.py:378

commit v4 on v3

--- a/solution.py
+++ b/solution.py
@@ -145,34 +145,7 @@
     )(*in_hbm(*args))
 
 
-def stage_kernel(*refs):
-    count = (len(refs) - 2) // 2
-    sources, dests, sems = refs[:count], refs[count + 1 : -1], refs[-1]
-    copies = [
-        pltpu.make_async_copy(src, dst, sems.at[i])
-        for i, (src, dst) in enumerate(zip(sources, dests))
-    ]
-    for copy in copies:
-        copy.start()
-    for copy in copies:
-        copy.wait()
-
-
-def stage(arrays, after):
-    vmem = pl.BlockSpec(memory_space=pltpu.VMEM)
-    anywhere = pl.BlockSpec(memory_space=pl.ANY)
-    return pl.pallas_call(
-        stage_kernel,
-        out_shape=tuple(jax.ShapeDtypeStruct(x.shape, x.dtype) for x in arrays),
-        in_specs=[anywhere] * (len(arrays) + 1),
-        out_specs=(vmem,) * len(arrays),
-        scratch_shapes=[pltpu.SemaphoreType.DMA((len(arrays),))],
-        compiler_params=pltpu.CompilerParams(vmem_limit_bytes=8 * MIB),
-        cost_estimate=pl.CostEstimate(flops=0, bytes_accessed=8 * MIB, transcendentals=0),
-    )(*in_hbm(*arrays), after)
-
-
-def base_kernel(which, p0, pa, pb, w_own, w_other, base_out):
+def base_kernel(which, p0, pa, pb, w_own, w_other, after, base_out):
     piece = p0.shape[0]
     cols = w_own.shape[1]
     rows = jnp.concatenate([p0[...], pa[...], pb[...]], axis=0)
@@ -181,20 +154,22 @@
         base_out[:, at] = jnp.dot(rows, w[...], preferred_element_type=f32).astype(bf16)
 
 
-def base_terms(which, pieces, w_own, w_other):
+def base_terms(which, pieces, w_own, w_other, after):
     count = sum(p.shape[0] for p in pieces)
     cols = w_own.shape[1]
     vmem = pl.BlockSpec(memory_space=pltpu.VMEM)
     return pl.pallas_call(
         base_kernel,
         out_shape=jax.ShapeDtypeStruct((count, 2 * cols), bf16),
-        in_specs=[pl.BlockSpec(memory_space=pltpu.SMEM)] + [vmem] * 5,
+        in_specs=[pl.BlockSpec(memory_space=pltpu.SMEM)]
+        + [vmem] * 5
+        + [pl.BlockSpec(memory_space=pl.ANY)],
         out_specs=vmem,
-        compiler_params=pltpu.CompilerParams(vmem_limit_bytes=8 * MIB),
+        compiler_params=pltpu.CompilerParams(vmem_limit_bytes=5 * MIB),
         cost_estimate=pl.CostEstimate(
             flops=4 * count * pieces[0].shape[1] * cols, bytes_accessed=2 * MIB, transcendentals=0
         ),
-    )(which, *pieces, w_own, w_other)
+    )(which, *pieces, w_own, w_other, after)
 
 
 def rank_kernel(
@@ -448,12 +423,11 @@
     which = jnp.stack([core, 1 - core])
     first = jnp.stack([home * kept, other * kept, (columns + y_here) * width, is_root])
 
-    (down_other,) = stage((down_other,), p0)
-    base_part = base_terms(which, (p0, pa, pb), output_weight, w_other)
+    base_part = base_terms(which, (p0, pa, pb), output_weight, w_other, down_other)
     packed = rank_terms(
         first, which, slots, (p0, pa, pb, p2), down, down_other, output_weight, w_other, base_part
     )
-    packs = [packed] + [along_x(packed, s) for s in (1, 3, 2)]
+    packs = [packed] + [along_x(packed, s) for s in (2, 1, 3)]
     sums = [base_part] + [to_root(base_part, s) for s in (2, 1, 3)]
     *ups, base = gather_ups(up, up_other, sums, packed)
     d2, spread = expand_last(first, slots, packs, *ups)

time: 89.3 us -> 88.5 us (level)
  waiting for transfers between devices: 30.1 us -> 32.7 us
  blocking collectives: 14.7 us -> 12.9 us
    all_to_all x1, blocking collectives: 14.7 us -> 12.9 us  [local(): lax.all_to_all(home_rows.reshape(NZ, mine_n, quarter), 'z', 0, 0, tiled=T...]
    ppermute x3, waiting for transfers between devices: 1.44 us -> 3.19 us  [along_x(): return lax.ppermute(x, 'x', [(i, (i + shift) % NX) for i in range(NX)])]
    pallas_call x1 -> x0, Pallas kernels: 1.6 us -> none  [stage(): pl.pallas_call(stage_kernel, out_shape=tuple((jax.ShapeDtypeStruct(x.shap...]
  transfers between devices with their start and end apart: 16 -> 16, of which waited for: 6 -> 7; matrix products, arithmetic and copies ran while one was open for 1% -> 1% of each run, Pallas kernels for 16% -> 16%
where the time goes in v4:
time: 88.5 us; the launch traced here: 88.1 us
  waiting for transfers between devices  32.7 us (37%)
  starting transfers between devices  25.1 us (28%)
  Pallas kernels  15.4 us (17%)
  blocking collectives  12.9 us (15%)
  other arithmetic  1.47 us (2%)
    ppermute x6, waiting for transfers between devices, along_y(): return lax.ppermute(x, ('y', 'c'), pairs)  17.7 us
    all_to_all x1, blocking collectives, local(): lax.all_to_all(home_rows.reshape(NZ, mine_n, quarter), 'z', 0, 0, tiled=T...  12.9 us
    all_to_all x1, waiting for transfers between devices, local(): p0 = lax.all_to_all(copies, 'z', 0, 0, tiled=True).reshape(block, features)  11.8 us
    all_to_all x1, starting transfers between devices, local(): p0 = lax.all_to_all(copies, 'z', 0, 0, tiled=True).reshape(block, features)  8.48 us
    ppermute x6, starting transfers between devices, along_y(): return lax.ppermute(x, ('y', 'c'), pairs)  8.36 us
    pallas_call x1, Pallas kernels, attend(): pl.pallas_call(attend_kernel, out_shape=jax.ShapeDtypeStruct((repeats, se...  5.77 us
    ppermute x3, starting transfers between devices, along_x(): return lax.ppermute(x, 'x', [(i, (i + shift) % NX) for i in range(NX)])  3.96 us
    ppermute x3, starting transfers between devices, to_root(): return lax.ppermute(x, ('z', 'x'), pairs)  3.72 us
  transfers between devices with their start and end apart: 16, of which 7 were waited for; matrix products, arithmetic and copies ran while one was open for 1% of the time, Pallas kernels for 16%

profile of v4, /device:TPU:6, one launch (start us, length us, event | category | flops | bytes accessed | tf_op | source)
XLA Modules:
  0.0 88.1 jit_solution(1210494955071532892)
XLA Ops:
  0.0 0.0 collective-permute-start.3
  0.0 0.5 collective-permute-start.8
  0.5 5.8 %shard_map.109 = bf16[8,8,2048]{2,1,0:T(8,128)(2,1)} custom-call(s32[8]{0:T(128)} %position.1, bf16[8,2048]{1,0:T(8,128)(2,1)} %query.1, bf16[8,256]{1,0:T(8,128)(2,1)} %fresh_key.1, bf16[8,256]{1,0:T(8,128)(2,1)} %fresh_value.1, bf16[8,1024,256]{2,1,0:T(8,128)(2,1)} %keys.1, bf16[8,1024,256]{2,1,0:T(8,128)(2,1)} %values.1), custom_call_target="tpu_custom_call" | custom-call | flops 134217728 | bytes 8388608 | tf_op jit(solution)/shard_map/pallas_call | solution.py:120
  6.3 8.5 %all-to-all-start = ((bf16[8,8,2048]{2,1,0:T(8,128)(2,1)}), bf16[8,8,2048]{2,1,0:T(8,128)(2,1)S(1)}, u32[]{:S(2)}, u32[]{:S(2)}) async-start(bf16[8,8,2048]{2,1,0:T(8,128)(2,1)} %shard_map.109), calls=%async_computation | async-start | bytes 524288 | tf_op jit(solution)/shard_map/all_to_all | solution.py:404
  14.8 0.1 collective-permute-start.4
  14.9 0.2 select_reduce_fusion
  15.2 11.8 %all-to-all-done = bf16[8,8,2048]{2,1,0:T(8,128)(2,1)S(1)} async-done(((bf16[8,8,2048]{2,1,0:T(8,128)(2,1)}), bf16[8,8,2048]{2,1,0:T(8,128)(2,1)S(1)}, u32[]{:S(2)}, u32[]{:S(2)}) %all-to-all-start) | async-done | bytes 262176 | tf_op jit(solution)/shard_map/all_to_all | solution.py:404
  27.0 1.6 %collective-permute-start = (bf16[64,2048]{1,0:T(8,128)(2,1)S(1)}, bf16[64,2048]{1,0:T(8,128)(2,1)}, u32[]{:S(2)}, u32[]{:S(2)}) collective-permute-start(bf16[64,2048]{1,0:T(8,128)(2,1)S(1)} %bitcast.18), channel_id=1, source_target_pairs={{0,8},{4,28},{8,16},{12,4},{16,24},{20,12},{24,0},{28,20},{1,9},{5... | collective-permute-start | bytes 786440 | tf_op jit(solution)/shard_map/ppermute | solution.py:353
  28.6 0.1 fusion.1
  28.6 0.1 reshape.130
  28.8 0.1 broadcast_in_dim.43
  28.9 0.1 iota_compare_fusion.1
  28.9 1.7 %collective-permute-start.1 = (bf16[64,2048]{1,0:T(8,128)(2,1)S(1)}, bf16[64,2048]{1,0:T(8,128)(2,1)}, u32[]{:S(2)}, u32[]{:S(2)}) collective-permute-start(bf16[64,2048]{1,0:T(8,128)(2,1)S(1)} %bitcast.19), channel_id=1, source_target_pairs={{0,24},{4,12},{8,0},{12,20},{16,8},{20,28},{24,16},{28,4},{1,25},{... | collective-permute-start | bytes 786440 | tf_op jit(solution)/shard_map/ppermute | solution.py:353
  30.6 5.9 %collective-permute-done.pa = bf16[64,2048]{1,0:T(8,128)(2,1)} collective-permute-done((bf16[64,2048]{1,0:T(8,128)(2,1)S(1)}, bf16[64,2048]{1,0:T(8,128)(2,1)}, u32[]{:S(2)}, u32[]{:S(2)}) %collective-permute-start) | collective-permute-done | bytes 262176 | tf_op jit(solution)/shard_map/ppermute | solution.py:353
  36.5 1.1 %collective-permute-start.2 = (bf16[64,2048]{1,0:T(8,128)(2,1)}, bf16[64,2048]{1,0:T(8,128)(2,1)}, u32[]{:S(2)}, u32[]{:S(2)}) collective-permute-start(bf16[64,2048]{1,0:T(8,128)(2,1)} %collective-permute-done.pa), channel_id=1, source_target_pairs={{0,8},{4,28},{8,16},{12,4},{16,24},{20,12},{24,0},{28,20},{1,9},{5... | collective-permute-start | bytes 786440 | tf_op jit(solution)/shard_map/ppermute | solution.py:353
  37.6 0.1 select_reduce_fusion.1
  37.7 0.1 reshape.131.slots
  37.8 0.1 pad_add_fusion.1.which
  37.9 0.1 pad_add_fusion.first
  37.9 0.0 collective-permute-done.4.w_other
  37.9 0.0 collective-permute-done.1.pb
  37.9 0.0 collective-permute-done.3.after.down_other
  38.0 1.7 %shard_map.110.after.b0 = bf16[192,256]{1,0:T(8,128)(2,1)S(1)} custom-call(s32[2]{0:T(128)S(1)} %pad_add_fusion.1.which, bf16[64,2048]{1,0:T(8,128)(2,1)S(1)} %bitcast.20, bf16[64,2048]{1,0:T(8,128)(2,1)} %collective-permute-done.pa, bf16[64,2048]{1,0:T(8,128)(2,1)} %collective-permute-done.1.pb, bf16[2048,128]{1,0:T(8,128)(2,1)S(1)} %copy-done, ...), custom_call_target="tpu_custom_call" | custom-call | flops 201326592 | bytes 2097152 | tf_op jit(solution)/shard_map/pallas_call | solution.py:161
  39.7 2.4 %collective-permute-start.10 = (bf16[192,256]{1,0:T(8,128)(2,1)S(1)}, bf16[192,256]{1,0:T(8,128)(2,1)S(1)}, u32[]{:S(2)}, u32[]{:S(2)}) collective-permute-start(bf16[192,256]{1,0:T(8,128)(2,1)S(1)} %shard_map.110.after.b0), channel_id=1, source_target_pairs={{3,0},{35,32},{64,65},{96,97},{129,130},{161,162},{194,195},{226,2... | collective-permute-start | bytes 294920 | tf_op jit(solution)/shard_map/ppermute | solution.py:361
  42.1 0.7 collective-permute-start.11
  42.7 0.7 collective-permute-start.9
  43.4 0.9 %collective-permute-done.2.p2 = bf16[64,2048]{1,0:T(8,128)(2,1)} collective-permute-done((bf16[64,2048]{1,0:T(8,128)(2,1)}, bf16[64,2048]{1,0:T(8,128)(2,1)}, u32[]{:S(2)}, u32[]{:S(2)}) %collective-permute-start.2) | collective-permute-done | bytes 262176 | tf_op jit(solution)/shard_map/ppermute | solution.py:353
  44.4 2.6 %shard_map.111.after.r0 = bf16[128,256]{1,0:T(8,128)(2,1)S(1)} custom-call(s32[4]{0:T(128)S(1)} %pad_add_fusion.first, s32[2]{0:T(128)S(1)} %pad_add_fusion.1.which, s32[1,256]{1,0:T(1,128)S(1)} %reshape.131.slots, bf16[64,2048]{1,0:T(8,128)(2,1)S(1)} %bitcast.21, bf16[64,2048]{1,0:T(8,128)(2,1)} %collective-permute-done.pa, ...), custom_call_target="tpu_custom_call" | custom-call | flops 1073741824 | bytes 6291456 | tf_op jit(solution)/shard_map/pallas_call | solution.py:207
  46.9 1.5 %collective-permute-start.5 = (bf16[128,256]{1,0:T(8,128)(2,1)S(1)}, bf16[128,256]{1,0:T(8,128)(2,1)S(1)}, u32[]{:S(2)}, u32[]{:S(2)}) collective-permute-start(bf16[128,256]{1,0:T(8,128)(2,1)S(1)} %shard_map.111.after.r0), channel_id=1, source_target_pairs={{0,2},{1,3},{2,0},{3,1},{4,6},{5,7},{6,4},{7,5},{8,10},{9,11},{10,... | collective-permute-start | bytes 196616 | tf_op jit(solution)/shard_map/ppermute | solution.py:365
  48.4 0.0 collective-permute-done.8.up_other
  48.4 2.5 %collective-permute-start.6 = (bf16[128,256]{1,0:T(8,128)(2,1)S(1)}, bf16[128,256]{1,0:T(8,128)(2,1)S(1)}, u32[]{:S(2)}, u32[]{:S(2)}) collective-permute-start(bf16[128,256]{1,0:T(8,128)(2,1)S(1)} %shard_map.111.after.r0), channel_id=1, source_target_pairs={{0,1},{1,2},{2,3},{3,0},{4,5},{5,6},{6,7},{7,4},{8,9},{9,10},{10,1... | collective-permute-start | bytes 196616 | tf_op jit(solution)/shard_map/ppermute | solution.py:365
  50.9 0.0 collective-permute-done.10.b2
  50.9 0.0 collective-permute-start.7
  50.9 0.0 collective-permute-done.9.b1
  50.9 2.2 %shard_map.112 = (bf16[512,2048]{1,0:T(8,128)(2,1)S(1)}, bf16[512,2048]{1,0:T(8,128)(2,1)S(1)}, f32[192,256]{1,0:T(8,128)S(1)}) custom-call(bf16[512,2048]{1,0:T(8,128)(2,1)} %bitcast.25, bf16[512,2048]{1,0:T(8,128)(2,1)} %collective-permute-done.8.up_other, bf16[192,256]{1,0:T(8,128)(2,1)S(1)} %shard_map.110.after.b0, ...), custom_call_target="tpu_custom_call" | custom-call | flops 1048576 | bytes 8388608 | tf_op jit(solution)/shard_map/pallas_call | solution.py:328
  53.2 3.2 %collective-permute-done.7.r3 = bf16[128,256]{1,0:T(8,128)(2,1)S(1)} collective-permute-done((bf16[128,256]{1,0:T(8,128)(2,1)S(1)}, bf16[128,256]{1,0:T(8,128)(2,1)S(1)}, u32[]{:S(2)}, u32[]{:S(2)}) %collective-permute-start.7) | collective-permute-done | bytes 65568 | tf_op jit(solution)/shard_map/ppermute | solution.py:365
  56.4 1.6 %shard_map.113 = (bf16[64,2048]{1,0:T(8,128)(2,1)S(1)}, bf16[192,1024]{1,0:T(8,128)(2,1)S(1)}) custom-call(s32[4]{0:T(128)S(1)} %pad_add_fusion.first, s32[1,256]{1,0:T(1,128)S(1)} %reshape.131.slots, bf16[128,256]{1,0:T(8,128)(2,1)S(1)} %shard_map.111.after.r0, bf16[128,256]{1,0:T(8,128)(2,1)S(1)} %collective-permute-done.5.r1, ...), custom_call_target="tpu_custom_call" | custom-call | flops 268435456 | bytes 4194304 | tf_op jit(solution)/shard_map/pallas_call | solution.py:268
  58.0 0.6 collective-permute-start.13
  58.5 1.5 %shard_map.114 = (bf16[64,2048]{1,0:T(8,128)(2,1)S(1)}, bf16[64,2048]{1,0:T(8,128)(2,1)S(1)}, bf16[64,2048]{1,0:T(8,128)(2,1)S(1)}) custom-call(s32[4]{0:T(128)S(1)} %pad_add_fusion.first, bf16[192,1024]{1,0:T(8,128)(2,1)S(1)} %get-tuple-element.15.spread, bf16[512,2048]{1,0:T(8,128)(2,1)S(1)} %get-tuple-element.13.up_own, ...), custom_call_target="tpu_custom_call" | custom-call | flops 805306368 | bytes 5242880 | tf_op jit(solution)/shard_map/pallas_call | solution.py:299
  60.1 3.0 %collective-permute-start.12 = (bf16[64,2048]{1,0:T(8,128)(2,1)S(1)}, bf16[64,2048]{1,0:T(8,128)(2,1)S(1)}, u32[]{:S(2)}, u32[]{:S(2)}) collective-permute-start(bf16[64,2048]{1,0:T(8,128)(2,1)S(1)} %get-tuple-element.18), channel_id=1, source_target_pairs={{0,24},{4,12},{8,0},{12,20},{16,8},{20,28},{24,16},{28,4},{1,25},{... | collective-permute-start | bytes 786440 | tf_op jit(solution)/shard_map/ppermute | solution.py:353
  63.1 3.6 %collective-permute-done.13 = bf16[64,2048]{1,0:T(8,128)(2,1)S(1)} collective-permute-done((bf16[64,2048]{1,0:T(8,128)(2,1)S(1)}, bf16[64,2048]{1,0:T(8,128)(2,1)S(1)}, u32[]{:S(2)}, u32[]{:S(2)}) %collective-permute-start.13) | collective-permute-done | bytes 262176 | tf_op jit(solution)/shard_map/ppermute | solution.py:353
  66.7 0.1 add_convert_fusion.1
  66.8 0.4 collective-permute-start.14
  67.2 1.9 %collective-permute-done.12 = bf16[64,2048]{1,0:T(8,128)(2,1)S(1)} collective-permute-done((bf16[64,2048]{1,0:T(8,128)(2,1)S(1)}, bf16[64,2048]{1,0:T(8,128)(2,1)S(1)}, u32[]{:S(2)}, u32[]{:S(2)}) %collective-permute-start.12) | collective-permute-done | bytes 262176 | tf_op jit(solution)/shard_map/ppermute | solution.py:353
  69.1 5.4 %collective-permute-done.14 = bf16[64,2048]{1,0:T(8,128)(2,1)S(1)} collective-permute-done((bf16[64,2048]{1,0:T(8,128)(2,1)S(1)}, bf16[64,2048]{1,0:T(8,128)(2,1)S(1)}, u32[]{:S(2)}, u32[]{:S(2)}) %collective-permute-start.14) | collective-permute-done | bytes 262176 | tf_op jit(solution)/shard_map/ppermute | solution.py:353
  74.5 0.1 fusion
  74.6 12.9 %all_to_all.10 = bf16[8,8,2048]{2,1,0:T(8,128)(2,1)S(1)} all-to-all(bf16[8,8,2048]{2,1,0:T(8,128)(2,1)S(1)} %fusion), channel_id=1, replica_groups=mesh['z'=8,'y'=4,'c'=2,'x'=4] {'z'}, dimensions={0} | all-to-all | bytes 524288 | tf_op jit(solution)/shard_map/all_to_all | solution.py:440
  87.5 0.7 reduce_sum.32
  (12 shorter events, 0.0 us)
Async XLA Ops:
  0.0 37.9 %collective-permute-start.3 = (bf16[8,64,2048]{2,1,0:T(8,128)(2,1)}, bf16[8,64,2048]{2,1,0:T(8,128)(2,1)S(1)}, u32[]{:S(2)}, u32[]{:S(2)}) collective-permute-start(bf16[8,64,2048]{2,1,0:T(8,128)(2,1)} %bitcast.22), channel_id=1, source_target_pairs={{0,4},{4,0},{1,5},{5,1},{2,6},{6,2},{3,7},{7,3},{8,12},{12,8},{9,1... | collective-permute-start | bytes 6291464 | tf_op jit(solution)/shard_map/ppermute | solution.py:344
  0.0 14.8 %copy-start = (bf16[2048,128]{1,0:T(8,128)(2,1)S(1)}, bf16[2048,128]{1,0:T(8,128)(2,1)}, u32[]{:S(2)}) copy-start(bf16[2048,128]{1,0:T(8,128)(2,1)} %w_own.3) | copy-start | bytes 1572868
  0.0 14.9 %copy-start.2 = (s32[512]{0:T(512)S(1)}, s32[512]{0:T(512)}, u32[]{:S(2)}) copy-start(s32[512]{0:T(512)} %param.18) | copy-start | bytes 6148
  0.0 14.9 %copy-start.3 = (s32[512]{0:T(512)S(1)}, s32[512]{0:T(512)}, u32[]{:S(2)}) copy-start(s32[512]{0:T(512)} %param.17) | copy-start | bytes 6148
  0.0 48.4 %collective-permute-start.8 = (bf16[512,2048]{1,0:T(8,128)(2,1)}, bf16[512,2048]{1,0:T(8,128)(2,1)}, u32[]{:S(2)}, u32[]{:S(2)}) collective-permute-start(bf16[512,2048]{1,0:T(8,128)(2,1)} %bitcast.24), channel_id=1, source_target_pairs={{0,4},{4,0},{1,5},{5,1},{2,6},{6,2},{3,7},{7,3},{8,12},{12,8},{9,1... | collective-permute-start | bytes 6291464 | tf_op jit(solution)/shard_map/ppermute | solution.py:344
  6.3 20.7 %all-to-all-start = ((bf16[8,8,2048]{2,1,0:T(8,128)(2,1)}), bf16[8,8,2048]{2,1,0:T(8,128)(2,1)S(1)}, u32[]{:S(2)}, u32[]{:S(2)}) async-start(bf16[8,8,2048]{2,1,0:T(8,128)(2,1)} %shard_map.109), calls=%async_computation | async-start | bytes 524288 | tf_op jit(solution)/shard_map/all_to_all | solution.py:404
  14.8 23.2 %collective-permute-start.4 = (bf16[2048,128]{1,0:T(8,128)(2,1)S(1)}, bf16[2048,128]{1,0:T(8,128)(2,1)S(1)}, u32[]{:S(2)}, u32[]{:S(2)}) collective-permute-start(bf16[2048,128]{1,0:T(8,128)(2,1)S(1)} %copy-done), channel_id=1, source_target_pairs={{0,4},{4,0},{1,5},{5,1},{2,6},{6,2},{3,7},{7,3},{8,12},{12,8},{9,1... | collective-permute-start | bytes 1572872 | tf_op jit(solution)/shard_map/ppermute | solution.py:344
  27.0 9.5 %collective-permute-start = (bf16[64,2048]{1,0:T(8,128)(2,1)S(1)}, bf16[64,2048]{1,0:T(8,128)(2,1)}, u32[]{:S(2)}, u32[]{:S(2)}) collective-permute-start(bf16[64,2048]{1,0:T(8,128)(2,1)S(1)} %bitcast.18), channel_id=1, source_target_pairs={{0,8},{4,28},{8,16},{12,4},{16,24},{20,12},{24,0},{28,20},{1,9},{5... | collective-permute-start | bytes 786440 | tf_op jit(solution)/shard_map/ppermute | solution.py:353
  28.9 9.0 %collective-permute-start.1 = (bf16[64,2048]{1,0:T(8,128)(2,1)S(1)}, bf16[64,2048]{1,0:T(8,128)(2,1)}, u32[]{:S(2)}, u32[]{:S(2)}) collective-permute-start(bf16[64,2048]{1,0:T(8,128)(2,1)S(1)} %bitcast.19), channel_id=1, source_target_pairs={{0,24},{4,12},{8,0},{12,20},{16,8},{20,28},{24,16},{28,4},{1,25},{... | collective-permute-start | bytes 786440 | tf_op jit(solution)/shard_map/ppermute | solution.py:353
  36.5 7.9 %collective-permute-start.2 = (bf16[64,2048]{1,0:T(8,128)(2,1)}, bf16[64,2048]{1,0:T(8,128)(2,1)}, u32[]{:S(2)}, u32[]{:S(2)}) collective-permute-start(bf16[64,2048]{1,0:T(8,128)(2,1)} %collective-permute-done.pa), channel_id=1, source_target_pairs={{0,8},{4,28},{8,16},{12,4},{16,24},{20,12},{24,0},{28,20},{1,9},{5... | collective-permute-start | bytes 786440 | tf_op jit(solution)/shard_map/ppermute | solution.py:353
  37.8 6.6 %copy-start.1 = (bf16[8,2048,64]{1,2,0:T(8,128)(2,1)S(1)}, bf16[8,2048,64]{1,2,0:T(8,128)(2,1)}, u32[]{:S(2)}) copy-start(bf16[8,2048,64]{1,2,0:T(8,128)(2,1)} %param.20) | copy-start | bytes 6291460
  39.7 11.2 %collective-permute-start.10 = (bf16[192,256]{1,0:T(8,128)(2,1)S(1)}, bf16[192,256]{1,0:T(8,128)(2,1)S(1)}, u32[]{:S(2)}, u32[]{:S(2)}) collective-permute-start(bf16[192,256]{1,0:T(8,128)(2,1)S(1)} %shard_map.110.after.b0), channel_id=1, source_target_pairs={{3,0},{35,32},{64,65},{96,97},{129,130},{161,162},{194,195},{226,2... | collective-permute-start | bytes 294920 | tf_op jit(solution)/shard_map/ppermute | solution.py:361
  42.1 8.8 %collective-permute-start.11 = (bf16[192,256]{1,0:T(8,128)(2,1)S(1)}, bf16[192,256]{1,0:T(8,128)(2,1)S(1)}, u32[]{:S(2)}, u32[]{:S(2)}) collective-permute-start(bf16[192,256]{1,0:T(8,128)(2,1)S(1)} %shard_map.110.after.b0), channel_id=1, source_target_pairs={{1,0},{33,32},{66,65},{98,97},{131,130},{163,162},{192,195},{224,2... | collective-permute-start | bytes 294920 | tf_op jit(solution)/shard_map/ppermute | solution.py:361
  42.7 8.2 %collective-permute-start.9 = (bf16[192,256]{1,0:T(8,128)(2,1)S(1)}, bf16[192,256]{1,0:T(8,128)(2,1)S(1)}, u32[]{:S(2)}, u32[]{:S(2)}) collective-permute-start(bf16[192,256]{1,0:T(8,128)(2,1)S(1)} %shard_map.110.after.b0), channel_id=1, source_target_pairs={{2,0},{34,32},{67,65},{99,97},{128,130},{160,162},{193,195},{225,2... | collective-permute-start | bytes 294920 | tf_op jit(solution)/shard_map/ppermute | solution.py:361
  46.9 6.2 %collective-permute-start.5 = (bf16[128,256]{1,0:T(8,128)(2,1)S(1)}, bf16[128,256]{1,0:T(8,128)(2,1)S(1)}, u32[]{:S(2)}, u32[]{:S(2)}) collective-permute-start(bf16[128,256]{1,0:T(8,128)(2,1)S(1)} %shard_map.111.after.r0), channel_id=1, source_target_pairs={{0,2},{1,3},{2,0},{3,1},{4,6},{5,7},{6,4},{7,5},{8,10},{9,11},{10,... | collective-permute-start | bytes 196616 | tf_op jit(solution)/shard_map/ppermute | solution.py:365
  48.4 4.7 %collective-permute-start.6 = (bf16[128,256]{1,0:T(8,128)(2,1)S(1)}, bf16[128,256]{1,0:T(8,128)(2,1)S(1)}, u32[]{:S(2)}, u32[]{:S(2)}) collective-permute-start(bf16[128,256]{1,0:T(8,128)(2,1)S(1)} %shard_map.111.after.r0), channel_id=1, source_target_pairs={{0,1},{1,2},{2,3},{3,0},{4,5},{5,6},{6,7},{7,4},{8,9},{9,10},{10,1... | collective-permute-start | bytes 196616 | tf_op jit(solution)/shard_map/ppermute | solution.py:365
  50.9 5.5 %collective-permute-start.7 = (bf16[128,256]{1,0:T(8,128)(2,1)S(1)}, bf16[128,256]{1,0:T(8,128)(2,1)S(1)}, u32[]{:S(2)}, u32[]{:S(2)}) collective-permute-start(bf16[128,256]{1,0:T(8,128)(2,1)S(1)} %shard_map.111.after.r0), channel_id=1, source_target_pairs={{0,3},{1,0},{2,1},{3,2},{4,7},{5,4},{6,5},{7,6},{8,11},{9,8},{10,9... | collective-permute-start | bytes 196616 | tf_op jit(solution)/shard_map/ppermute | solution.py:365
  58.0 8.8 %collective-permute-start.13 = (bf16[64,2048]{1,0:T(8,128)(2,1)S(1)}, bf16[64,2048]{1,0:T(8,128)(2,1)S(1)}, u32[]{:S(2)}, u32[]{:S(2)}) collective-permute-start(bf16[64,2048]{1,0:T(8,128)(2,1)S(1)} %get-tuple-element.20), channel_id=1, source_target_pairs={{0,8},{4,28},{8,16},{12,4},{16,24},{20,12},{24,0},{28,20},{1,9},{5... | collective-permute-start | bytes 786440 | tf_op jit(solution)/shard_map/ppermute | solution.py:353
  60.1 9.0 %collective-permute-start.12 = (bf16[64,2048]{1,0:T(8,128)(2,1)S(1)}, bf16[64,2048]{1,0:T(8,128)(2,1)S(1)}, u32[]{:S(2)}, u32[]{:S(2)}) collective-permute-start(bf16[64,2048]{1,0:T(8,128)(2,1)S(1)} %get-tuple-element.18), channel_id=1, source_target_pairs={{0,24},{4,12},{8,0},{12,20},{16,8},{20,28},{24,16},{28,4},{1,25},{... | collective-permute-start | bytes 786440 | tf_op jit(solution)/shard_map/ppermute | solution.py:353
  66.8 7.7 %collective-permute-start.14 = (bf16[64,2048]{1,0:T(8,128)(2,1)S(1)}, bf16[64,2048]{1,0:T(8,128)(2,1)S(1)}, u32[]{:S(2)}, u32[]{:S(2)}) collective-permute-start(bf16[64,2048]{1,0:T(8,128)(2,1)S(1)} %add_convert_fusion.1), channel_id=1, source_target_pairs={{0,8},{4,28},{8,16},{12,4},{16,24},{20,12},{24,0},{28,20},{1,9},{5... | collective-permute-start | bytes 786440 | tf_op jit(solution)/shard_map/ppermute | solution.py:353

commit v5 on v4

--- a/solution.py
+++ b/solution.py
@@ -231,12 +231,14 @@
             o[:, cols] = delta[k * piece : (k + 1) * piece, :]
 
 
-def expand_last_kernel(first, slots, r0, r1, r2, r3, up_own, up_other, o2, spread, spread2):
+def expand_kernel(
+    first, slots, r0, r1, r2, r3, up_own, up_other, base, o0, oa, ob, o2, spread
+):
+    outs = (o0, oa, ob, o2)
     count = slots.shape[1]
     kept_rank = up_own.shape[0]
     piece = o2.shape[0]
     rank = r0.shape[0] - piece
-    head = count - piece
     summed = (r0[...].astype(f32) + r1[...].astype(f32)) + (
         r2[...].astype(f32) + r3[...].astype(f32)
     )
@@ -248,64 +250,34 @@
         for j in range(kept_rank // LANES):
             slot = (first[which] + 2 * j + part).astype(f32)
             at = which * kept_rank + j * LANES
-            block = jnp.where(slot_rows == slot, both, 0.0).astype(bf16)
-            spread[:, at : at + LANES] = block[:head, :]
-            spread2[:, at : at + LANES] = block[head:, :]
-    scaled_rows(spread2, up_own, up_other, (o2,))
+            spread[:, at : at + LANES] = jnp.where(slot_rows == slot, both, 0.0).astype(bf16)
+    scaled_rows(spread, up_own, up_other, outs)
 
     @pl.when(first[3] == 1)
     def _():
         at = pl.ds(pl.multiple_of(first[2], LANES), count)
         o2[:, at] = (o2[:, at].astype(f32) + summed[rank:, :]).astype(bf16)
-
-
-def expand_last(first, slots, ranks, up_own, up_other):
+        for k, o in enumerate((o0, oa, ob)):
+            o[:, at] = (o[:, at].astype(f32) + base[k * piece : (k + 1) * piece, :]).astype(bf16)
+
+
+def expand(first, slots, ranks, up_own, up_other, base):
     count = slots.shape[1]
     kept_rank, quarter = up_own.shape
     piece = count // NY
     vmem = pl.BlockSpec(memory_space=pltpu.VMEM)
     smem = pl.BlockSpec(memory_space=pltpu.SMEM)
     return pl.pallas_call(
-        expand_last_kernel,
-        out_shape=(
-            jax.ShapeDtypeStruct((piece, quarter), bf16),
-            jax.ShapeDtypeStruct((count - piece, 2 * kept_rank), bf16),
-        ),
-        in_specs=[smem] + [vmem] * 7,
-        out_specs=(vmem,) * 2,
-        scratch_shapes=[pltpu.VMEM((piece, 2 * kept_rank), bf16)],
-        compiler_params=pltpu.CompilerParams(vmem_limit_bytes=10 * MIB),
+        expand_kernel,
+        out_shape=(jax.ShapeDtypeStruct((piece, quarter), bf16),) * NY,
+        in_specs=[smem] + [vmem] * 8,
+        out_specs=(vmem,) * NY,
+        scratch_shapes=[pltpu.VMEM((count, 2 * kept_rank), bf16)],
+        compiler_params=pltpu.CompilerParams(vmem_limit_bytes=12 * MIB),
         cost_estimate=pl.CostEstimate(
-            flops=4 * piece * kept_rank * quarter, bytes_accessed=4 * MIB, transcendentals=0
-        ),
-    )(first, slots, *ranks, up_own, up_other)
-
-
-def expand_kernel(first, spread, up_own, up_other, base, *outs):
-    scaled_rows(spread, up_own, up_other, outs)
-
-    @pl.when(first[3] == 1)
-    def _():
-        piece = outs[0].shape[0]
-        at = pl.ds(pl.multiple_of(first[2], LANES), base.shape[1])
-        for k, o in enumerate(outs):
-            o[:, at] = (o[:, at].astype(f32) + base[k * piece : (k + 1) * piece, :]).astype(bf16)
-
-
-def expand(first, spread, up_own, up_other, base):
-    quarter = up_own.shape[1]
-    piece = spread.shape[0] // (NY - 1)
-    vmem = pl.BlockSpec(memory_space=pltpu.VMEM)
-    return pl.pallas_call(
-        expand_kernel,
-        out_shape=(jax.ShapeDtypeStruct((piece, quarter), bf16),) * (NY - 1),
-        in_specs=[pl.BlockSpec(memory_space=pltpu.SMEM)] + [vmem] * 4,
-        out_specs=(vmem,) * (NY - 1),
-        compiler_params=pltpu.CompilerParams(vmem_limit_bytes=10 * MIB),
-        cost_estimate=pl.CostEstimate(
-            flops=2 * spread.size * quarter, bytes_accessed=5 * MIB, transcendentals=0
-        ),
-    )(first, spread, up_own, up_other, base)
+            flops=4 * count * kept_rank * quarter, bytes_accessed=6 * MIB, transcendentals=0
+        ),
+    )(first, slots, *ranks, up_own, up_other, base)
 
 
 def gather_kernel(up_own, up_other, b0, b1, b2, b3, after, own_out, other_out, base_out, sems):
@@ -430,9 +402,8 @@
     packs = [packed] + [along_x(packed, s) for s in (2, 1, 3)]
     sums = [base_part] + [to_root(base_part, s) for s in (2, 1, 3)]
     *ups, base = gather_ups(up, up_other, sums, packed)
-    d2, spread = expand_last(first, slots, packs, *ups)
+    d0, da, db, d2 = expand(first, slots, packs, *ups, base)
     e2 = along_y(d2, 1)
-    d0, da, db = expand(first, spread, *ups, base)
 
     ea = along_y(da, -1)
     eb = along_y(add(db, e2), 1)

time: 88.5 us -> 87.8 us (level)
  Pallas kernels: 15.4 us -> 14.4 us
  waiting for transfers between devices: 32.7 us -> 33.7 us
    pallas_call x1 -> x0, Pallas kernels: 1.62 us -> none  [expand_last(): pl.pallas_call(expand_last_kernel, out_shape=(jax.ShapeDtypeStruct((piece...]
    ppermute x6, waiting for transfers between devices: 17.7 us -> 18.7 us  [along_y(): return lax.ppermute(x, ('y', 'c'), pairs)]
  transfers between devices with their start and end apart: 16 -> 16, of which waited for: 7 -> 7; matrix products, arithmetic and copies ran while one was open for 1% -> 1% of each run, Pallas kernels for 16% -> 14%
where the time goes in v5:
time: 87.8 us; the launch traced here: 87.5 us
  waiting for transfers between devices  33.7 us (38%)
  starting transfers between devices  24.5 us (28%)
  Pallas kernels  14.4 us (16%)
  blocking collectives  12.9 us (15%)
  other arithmetic  1.47 us (2%)
    ppermute x6, waiting for transfers between devices, along_y(): return lax.ppermute(x, ('y', 'c'), pairs)  18.7 us
    all_to_all x1, blocking collectives, local(): lax.all_to_all(home_rows.reshape(NZ, mine_n, quarter), 'z', 0, 0, tiled=T...  12.9 us
    all_to_all x1, waiting for transfers between devices, local(): p0 = lax.all_to_all(copies, 'z', 0, 0, tiled=True).reshape(block, features)  11.8 us
    all_to_all x1, starting transfers between devices, local(): p0 = lax.all_to_all(copies, 'z', 0, 0, tiled=True).reshape(block, features)  8.48 us
    ppermute x6, starting transfers between devices, along_y(): return lax.ppermute(x, ('y', 'c'), pairs)  7.78 us
    pallas_call x1, Pallas kernels, attend(): pl.pallas_call(attend_kernel, out_shape=jax.ShapeDtypeStruct((repeats, se...  5.78 us
    ppermute x3, starting transfers between devices, along_x(): return lax.ppermute(x, 'x', [(i, (i + shift) % NX) for i in range(NX)])  3.95 us
    ppermute x3, starting transfers between devices, to_root(): return lax.ppermute(x, ('z', 'x'), pairs)  3.72 us
  transfers between devices with their start and end apart: 16, of which 7 were waited for; matrix products, arithmetic and copies ran while one was open for 1% of the time, Pallas kernels for 14%

profile of v5, /device:TPU:6, one launch (start us, length us, event | category | flops | bytes accessed | tf_op | source)
XLA Modules:
  0.0 87.5 jit_solution(11273799077190981293)
XLA Ops:
  0.0 0.0 collective-permute-start.3
  0.0 0.5 collective-permute-start.8
  0.5 5.8 %shard_map.109 = bf16[8,8,2048]{2,1,0:T(8,128)(2,1)} custom-call(s32[8]{0:T(128)} %position.1, bf16[8,2048]{1,0:T(8,128)(2,1)} %query.1, bf16[8,256]{1,0:T(8,128)(2,1)} %fresh_key.1, bf16[8,256]{1,0:T(8,128)(2,1)} %fresh_value.1, bf16[8,1024,256]{2,1,0:T(8,128)(2,1)} %keys.1, bf16[8,1024,256]{2,1,0:T(8,128)(2,1)} %values.1), custom_call_target="tpu_custom_call" | custom-call | flops 134217728 | bytes 8388608 | tf_op jit(solution)/shard_map/pallas_call | solution.py:120
  6.3 8.5 %all-to-all-start = ((bf16[8,8,2048]{2,1,0:T(8,128)(2,1)}), bf16[8,8,2048]{2,1,0:T(8,128)(2,1)S(1)}, u32[]{:S(2)}, u32[]{:S(2)}) async-start(bf16[8,8,2048]{2,1,0:T(8,128)(2,1)} %shard_map.109), calls=%async_computation | async-start | bytes 524288 | tf_op jit(solution)/shard_map/all_to_all | solution.py:376
  14.8 0.1 collective-permute-start.4
  14.9 0.2 select_reduce_fusion
  15.2 11.8 %all-to-all-done = bf16[8,8,2048]{2,1,0:T(8,128)(2,1)S(1)} async-done(((bf16[8,8,2048]{2,1,0:T(8,128)(2,1)}), bf16[8,8,2048]{2,1,0:T(8,128)(2,1)S(1)}, u32[]{:S(2)}, u32[]{:S(2)}) %all-to-all-start) | async-done | bytes 262176 | tf_op jit(solution)/shard_map/all_to_all | solution.py:376
  27.0 1.6 %collective-permute-start = (bf16[64,2048]{1,0:T(8,128)(2,1)S(1)}, bf16[64,2048]{1,0:T(8,128)(2,1)}, u32[]{:S(2)}, u32[]{:S(2)}) collective-permute-start(bf16[64,2048]{1,0:T(8,128)(2,1)S(1)} %bitcast.18), channel_id=1, source_target_pairs={{0,8},{4,28},{8,16},{12,4},{16,24},{20,12},{24,0},{28,20},{1,9},{5... | collective-permute-start | bytes 786440 | tf_op jit(solution)/shard_map/ppermute | solution.py:325
  28.6 0.1 fusion.1
  28.7 0.1 reshape.130
  28.8 0.1 broadcast_in_dim.43
  28.9 0.1 iota_compare_fusion.1
  28.9 1.7 %collective-permute-start.1 = (bf16[64,2048]{1,0:T(8,128)(2,1)S(1)}, bf16[64,2048]{1,0:T(8,128)(2,1)}, u32[]{:S(2)}, u32[]{:S(2)}) collective-permute-start(bf16[64,2048]{1,0:T(8,128)(2,1)S(1)} %bitcast.19), channel_id=1, source_target_pairs={{0,24},{4,12},{8,0},{12,20},{16,8},{20,28},{24,16},{28,4},{1,25},{... | collective-permute-start | bytes 786440 | tf_op jit(solution)/shard_map/ppermute | solution.py:325
  30.6 5.9 %collective-permute-done.pa = bf16[64,2048]{1,0:T(8,128)(2,1)} collective-permute-done((bf16[64,2048]{1,0:T(8,128)(2,1)S(1)}, bf16[64,2048]{1,0:T(8,128)(2,1)}, u32[]{:S(2)}, u32[]{:S(2)}) %collective-permute-start) | collective-permute-done | bytes 262176 | tf_op jit(solution)/shard_map/ppermute | solution.py:325
  36.5 1.1 %collective-permute-start.2 = (bf16[64,2048]{1,0:T(8,128)(2,1)}, bf16[64,2048]{1,0:T(8,128)(2,1)}, u32[]{:S(2)}, u32[]{:S(2)}) collective-permute-start(bf16[64,2048]{1,0:T(8,128)(2,1)} %collective-permute-done.pa), channel_id=1, source_target_pairs={{0,8},{4,28},{8,16},{12,4},{16,24},{20,12},{24,0},{28,20},{1,9},{5... | collective-permute-start | bytes 786440 | tf_op jit(solution)/shard_map/ppermute | solution.py:325
  37.6 0.1 select_reduce_fusion.1
  37.7 0.1 reshape.131.slots
  37.8 0.1 pad_add_fusion.1.which
  37.9 0.1 pad_add_fusion.first
  37.9 0.0 collective-permute-done.4.w_other
  38.0 0.0 collective-permute-done.1.pb
  38.0 0.0 collective-permute-done.3.after.down_other
  38.0 1.7 %shard_map.110.after.b0 = bf16[192,256]{1,0:T(8,128)(2,1)S(1)} custom-call(s32[2]{0:T(128)S(1)} %pad_add_fusion.1.which, bf16[64,2048]{1,0:T(8,128)(2,1)S(1)} %bitcast.20, bf16[64,2048]{1,0:T(8,128)(2,1)} %collective-permute-done.pa, bf16[64,2048]{1,0:T(8,128)(2,1)} %collective-permute-done.1.pb, bf16[2048,128]{1,0:T(8,128)(2,1)S(1)} %copy-done, ...), custom_call_target="tpu_custom_call" | custom-call | flops 201326592 | bytes 2097152 | tf_op jit(solution)/shard_map/pallas_call | solution.py:161
  39.7 2.4 %collective-permute-start.10 = (bf16[192,256]{1,0:T(8,128)(2,1)S(1)}, bf16[192,256]{1,0:T(8,128)(2,1)S(1)}, u32[]{:S(2)}, u32[]{:S(2)}) collective-permute-start(bf16[192,256]{1,0:T(8,128)(2,1)S(1)} %shard_map.110.after.b0), channel_id=1, source_target_pairs={{3,0},{35,32},{64,65},{96,97},{129,130},{161,162},{194,195},{226,2... | collective-permute-start | bytes 294920 | tf_op jit(solution)/shard_map/ppermute | solution.py:333
  42.1 0.7 collective-permute-start.11
  42.8 0.7 collective-permute-start.9
  43.4 0.9 %collective-permute-done.2.p2 = bf16[64,2048]{1,0:T(8,128)(2,1)} collective-permute-done((bf16[64,2048]{1,0:T(8,128)(2,1)}, bf16[64,2048]{1,0:T(8,128)(2,1)}, u32[]{:S(2)}, u32[]{:S(2)}) %collective-permute-start.2) | collective-permute-done | bytes 262176 | tf_op jit(solution)/shard_map/ppermute | solution.py:325
  44.4 2.6 %shard_map.111.after.r0 = bf16[128,256]{1,0:T(8,128)(2,1)S(1)} custom-call(s32[4]{0:T(128)S(1)} %pad_add_fusion.first, s32[2]{0:T(128)S(1)} %pad_add_fusion.1.which, s32[1,256]{1,0:T(1,128)S(1)} %reshape.131.slots, bf16[64,2048]{1,0:T(8,128)(2,1)S(1)} %bitcast.21, bf16[64,2048]{1,0:T(8,128)(2,1)} %collective-permute-done.pa, ...), custom_call_target="tpu_custom_call" | custom-call | flops 1073741824 | bytes 6291456 | tf_op jit(solution)/shard_map/pallas_call | solution.py:207
  46.9 1.5 %collective-permute-start.5 = (bf16[128,256]{1,0:T(8,128)(2,1)S(1)}, bf16[128,256]{1,0:T(8,128)(2,1)S(1)}, u32[]{:S(2)}, u32[]{:S(2)}) collective-permute-start(bf16[128,256]{1,0:T(8,128)(2,1)S(1)} %shard_map.111.after.r0), channel_id=1, source_target_pairs={{0,2},{1,3},{2,0},{3,1},{4,6},{5,7},{6,4},{7,5},{8,10},{9,11},{10,... | collective-permute-start | bytes 196616 | tf_op jit(solution)/shard_map/ppermute | solution.py:337
  48.4 0.0 collective-permute-done.8.up_other
  48.4 2.5 %collective-permute-start.6 = (bf16[128,256]{1,0:T(8,128)(2,1)S(1)}, bf16[128,256]{1,0:T(8,128)(2,1)S(1)}, u32[]{:S(2)}, u32[]{:S(2)}) collective-permute-start(bf16[128,256]{1,0:T(8,128)(2,1)S(1)} %shard_map.111.after.r0), channel_id=1, source_target_pairs={{0,1},{1,2},{2,3},{3,0},{4,5},{5,6},{6,7},{7,4},{8,9},{9,10},{10,1... | collective-permute-start | bytes 196616 | tf_op jit(solution)/shard_map/ppermute | solution.py:337
  50.9 0.0 collective-permute-done.10.b2
  50.9 0.0 collective-permute-start.7
  50.9 0.0 collective-permute-done.9.b1
  50.9 2.2 %shard_map.112 = (bf16[512,2048]{1,0:T(8,128)(2,1)S(1)}, bf16[512,2048]{1,0:T(8,128)(2,1)S(1)}, f32[192,256]{1,0:T(8,128)S(1)}) custom-call(bf16[512,2048]{1,0:T(8,128)(2,1)} %bitcast.25, bf16[512,2048]{1,0:T(8,128)(2,1)} %collective-permute-done.8.up_other, bf16[192,256]{1,0:T(8,128)(2,1)S(1)} %shard_map.110.after.b0, ...), custom_call_target="tpu_custom_call" | custom-call | flops 1048576 | bytes 8388608 | tf_op jit(solution)/shard_map/pallas_call | solution.py:300
  53.2 0.0 collective-permute-done.5.r1
  53.2 3.2 %collective-permute-done.7.r3 = bf16[128,256]{1,0:T(8,128)(2,1)S(1)} collective-permute-done((bf16[128,256]{1,0:T(8,128)(2,1)S(1)}, bf16[128,256]{1,0:T(8,128)(2,1)S(1)}, u32[]{:S(2)}, u32[]{:S(2)}) %collective-permute-start.7) | collective-permute-done | bytes 65568 | tf_op jit(solution)/shard_map/ppermute | solution.py:337
  56.4 2.1 %shard_map.113 = (bf16[64,2048]{1,0:T(8,128)(2,1)S(1)}, bf16[64,2048]{1,0:T(8,128)(2,1)S(1)}, bf16[64,2048]{1,0:T(8,128)(2,1)S(1)}, bf16[64,2048]{1,0:T(8,128)(2,1)S(1)}) custom-call(s32[4]{0:T(128)S(1)} %pad_add_fusion.first, s32[1,256]{1,0:T(1,128)S(1)} %reshape.131.slots, bf16[128,256]{1,0:T(8,128)(2,1)S(1)} %shard_map.111.after.r0, ...), custom_call_target="tpu_custom_call" | custom-call | flops 1073741824 | bytes 6291456 | tf_op jit(solution)/shard_map/pallas_call | solution.py:270
  58.5 0.4 collective-permute-start.13
  58.8 2.9 %collective-permute-start.12 = (bf16[64,2048]{1,0:T(8,128)(2,1)S(1)}, bf16[64,2048]{1,0:T(8,128)(2,1)S(1)}, u32[]{:S(2)}, u32[]{:S(2)}) collective-permute-start(bf16[64,2048]{1,0:T(8,128)(2,1)S(1)} %get-tuple-element.16), channel_id=1, source_target_pairs={{0,24},{4,12},{8,0},{12,20},{16,8},{20,28},{24,16},{28,4},{1,25},{... | collective-permute-start | bytes 786440 | tf_op jit(solution)/shard_map/ppermute | solution.py:325
  61.8 4.3 %collective-permute-done.13 = bf16[64,2048]{1,0:T(8,128)(2,1)S(1)} collective-permute-done((bf16[64,2048]{1,0:T(8,128)(2,1)S(1)}, bf16[64,2048]{1,0:T(8,128)(2,1)S(1)}, u32[]{:S(2)}, u32[]{:S(2)}) %collective-permute-start.13) | collective-permute-done | bytes 262176 | tf_op jit(solution)/shard_map/ppermute | solution.py:325
  66.1 0.1 add_convert_fusion.1
  66.2 0.1 collective-permute-start.14
  66.3 2.1 %collective-permute-done.12 = bf16[64,2048]{1,0:T(8,128)(2,1)S(1)} collective-permute-done((bf16[64,2048]{1,0:T(8,128)(2,1)S(1)}, bf16[64,2048]{1,0:T(8,128)(2,1)S(1)}, u32[]{:S(2)}, u32[]{:S(2)}) %collective-permute-start.12) | collective-permute-done | bytes 262176 | tf_op jit(solution)/shard_map/ppermute | solution.py:325
  68.4 5.5 %collective-permute-done.14 = bf16[64,2048]{1,0:T(8,128)(2,1)S(1)} collective-permute-done((bf16[64,2048]{1,0:T(8,128)(2,1)S(1)}, bf16[64,2048]{1,0:T(8,128)(2,1)S(1)}, u32[]{:S(2)}, u32[]{:S(2)}) %collective-permute-start.14) | collective-permute-done | bytes 262176 | tf_op jit(solution)/shard_map/ppermute | solution.py:325
  73.9 0.1 fusion
  74.0 12.9 %all_to_all.10 = bf16[8,8,2048]{2,1,0:T(8,128)(2,1)S(1)} all-to-all(bf16[8,8,2048]{2,1,0:T(8,128)(2,1)S(1)} %fusion), channel_id=1, replica_groups=mesh['z'=8,'y'=4,'c'=2,'x'=4] {'z'}, dimensions={0} | all-to-all | bytes 524288 | tf_op jit(solution)/shard_map/all_to_all | solution.py:411
  86.8 0.7 reduce_sum.32
  (11 shorter events, 0.0 us)
Async XLA Ops:
  0.0 38.0 %collective-permute-start.3 = (bf16[8,64,2048]{2,1,0:T(8,128)(2,1)}, bf16[8,64,2048]{2,1,0:T(8,128)(2,1)S(1)}, u32[]{:S(2)}, u32[]{:S(2)}) collective-permute-start(bf16[8,64,2048]{2,1,0:T(8,128)(2,1)} %bitcast.22), channel_id=1, source_target_pairs={{0,4},{4,0},{1,5},{5,1},{2,6},{6,2},{3,7},{7,3},{8,12},{12,8},{9,1... | collective-permute-start | bytes 6291464 | tf_op jit(solution)/shard_map/ppermute | solution.py:316
  0.0 14.8 %copy-start = (bf16[2048,128]{1,0:T(8,128)(2,1)S(1)}, bf16[2048,128]{1,0:T(8,128)(2,1)}, u32[]{:S(2)}) copy-start(bf16[2048,128]{1,0:T(8,128)(2,1)} %w_own.3) | copy-start | bytes 1572868
  0.0 14.9 %copy-start.2 = (s32[512]{0:T(512)S(1)}, s32[512]{0:T(512)}, u32[]{:S(2)}) copy-start(s32[512]{0:T(512)} %param.18) | copy-start | bytes 6148
  0.0 14.9 %copy-start.3 = (s32[512]{0:T(512)S(1)}, s32[512]{0:T(512)}, u32[]{:S(2)}) copy-start(s32[512]{0:T(512)} %param.17) | copy-start | bytes 6148
  0.0 48.4 %collective-permute-start.8 = (bf16[512,2048]{1,0:T(8,128)(2,1)}, bf16[512,2048]{1,0:T(8,128)(2,1)}, u32[]{:S(2)}, u32[]{:S(2)}) collective-permute-start(bf16[512,2048]{1,0:T(8,128)(2,1)} %bitcast.24), channel_id=1, source_target_pairs={{0,4},{4,0},{1,5},{5,1},{2,6},{6,2},{3,7},{7,3},{8,12},{12,8},{9,1... | collective-permute-start | bytes 6291464 | tf_op jit(solution)/shard_map/ppermute | solution.py:316
  6.3 20.7 %all-to-all-start = ((bf16[8,8,2048]{2,1,0:T(8,128)(2,1)}), bf16[8,8,2048]{2,1,0:T(8,128)(2,1)S(1)}, u32[]{:S(2)}, u32[]{:S(2)}) async-start(bf16[8,8,2048]{2,1,0:T(8,128)(2,1)} %shard_map.109), calls=%async_computation | async-start | bytes 524288 | tf_op jit(solution)/shard_map/all_to_all | solution.py:376
  14.8 23.2 %collective-permute-start.4 = (bf16[2048,128]{1,0:T(8,128)(2,1)S(1)}, bf16[2048,128]{1,0:T(8,128)(2,1)S(1)}, u32[]{:S(2)}, u32[]{:S(2)}) collective-permute-start(bf16[2048,128]{1,0:T(8,128)(2,1)S(1)} %copy-done), channel_id=1, source_target_pairs={{0,4},{4,0},{1,5},{5,1},{2,6},{6,2},{3,7},{7,3},{8,12},{12,8},{9,1... | collective-permute-start | bytes 1572872 | tf_op jit(solution)/shard_map/ppermute | solution.py:316
  27.0 9.5 %collective-permute-start = (bf16[64,2048]{1,0:T(8,128)(2,1)S(1)}, bf16[64,2048]{1,0:T(8,128)(2,1)}, u32[]{:S(2)}, u32[]{:S(2)}) collective-permute-start(bf16[64,2048]{1,0:T(8,128)(2,1)S(1)} %bitcast.18), channel_id=1, source_target_pairs={{0,8},{4,28},{8,16},{12,4},{16,24},{20,12},{24,0},{28,20},{1,9},{5... | collective-permute-start | bytes 786440 | tf_op jit(solution)/shard_map/ppermute | solution.py:325
  28.9 9.0 %collective-permute-start.1 = (bf16[64,2048]{1,0:T(8,128)(2,1)S(1)}, bf16[64,2048]{1,0:T(8,128)(2,1)}, u32[]{:S(2)}, u32[]{:S(2)}) collective-permute-start(bf16[64,2048]{1,0:T(8,128)(2,1)S(1)} %bitcast.19), channel_id=1, source_target_pairs={{0,24},{4,12},{8,0},{12,20},{16,8},{20,28},{24,16},{28,4},{1,25},{... | collective-permute-start | bytes 786440 | tf_op jit(solution)/shard_map/ppermute | solution.py:325
  36.5 7.9 %collective-permute-start.2 = (bf16[64,2048]{1,0:T(8,128)(2,1)}, bf16[64,2048]{1,0:T(8,128)(2,1)}, u32[]{:S(2)}, u32[]{:S(2)}) collective-permute-start(bf16[64,2048]{1,0:T(8,128)(2,1)} %collective-permute-done.pa), channel_id=1, source_target_pairs={{0,8},{4,28},{8,16},{12,4},{16,24},{20,12},{24,0},{28,20},{1,9},{5... | collective-permute-start | bytes 786440 | tf_op jit(solution)/shard_map/ppermute | solution.py:325
  37.8 6.6 %copy-start.1 = (bf16[8,2048,64]{1,2,0:T(8,128)(2,1)S(1)}, bf16[8,2048,64]{1,2,0:T(8,128)(2,1)}, u32[]{:S(2)}) copy-start(bf16[8,2048,64]{1,2,0:T(8,128)(2,1)} %param.20) | copy-start | bytes 6291460
  39.7 11.2 %collective-permute-start.10 = (bf16[192,256]{1,0:T(8,128)(2,1)S(1)}, bf16[192,256]{1,0:T(8,128)(2,1)S(1)}, u32[]{:S(2)}, u32[]{:S(2)}) collective-permute-start(bf16[192,256]{1,0:T(8,128)(2,1)S(1)} %shard_map.110.after.b0), channel_id=1, source_target_pairs={{3,0},{35,32},{64,65},{96,97},{129,130},{161,162},{194,195},{226,2... | collective-permute-start | bytes 294920 | tf_op jit(solution)/shard_map/ppermute | solution.py:333
  42.1 8.8 %collective-permute-start.11 = (bf16[192,256]{1,0:T(8,128)(2,1)S(1)}, bf16[192,256]{1,0:T(8,128)(2,1)S(1)}, u32[]{:S(2)}, u32[]{:S(2)}) collective-permute-start(bf16[192,256]{1,0:T(8,128)(2,1)S(1)} %shard_map.110.after.b0), channel_id=1, source_target_pairs={{1,0},{33,32},{66,65},{98,97},{131,130},{163,162},{192,195},{224,2... | collective-permute-start | bytes 294920 | tf_op jit(solution)/shard_map/ppermute | solution.py:333
  42.8 8.2 %collective-permute-start.9 = (bf16[192,256]{1,0:T(8,128)(2,1)S(1)}, bf16[192,256]{1,0:T(8,128)(2,1)S(1)}, u32[]{:S(2)}, u32[]{:S(2)}) collective-permute-start(bf16[192,256]{1,0:T(8,128)(2,1)S(1)} %shard_map.110.after.b0), channel_id=1, source_target_pairs={{2,0},{34,32},{67,65},{99,97},{128,130},{160,162},{193,195},{225,2... | collective-permute-start | bytes 294920 | tf_op jit(solution)/shard_map/ppermute | solution.py:333
  46.9 6.2 %collective-permute-start.5 = (bf16[128,256]{1,0:T(8,128)(2,1)S(1)}, bf16[128,256]{1,0:T(8,128)(2,1)S(1)}, u32[]{:S(2)}, u32[]{:S(2)}) collective-permute-start(bf16[128,256]{1,0:T(8,128)(2,1)S(1)} %shard_map.111.after.r0), channel_id=1, source_target_pairs={{0,2},{1,3},{2,0},{3,1},{4,6},{5,7},{6,4},{7,5},{8,10},{9,11},{10,... | collective-permute-start | bytes 196616 | tf_op jit(solution)/shard_map/ppermute | solution.py:337
  48.4 4.7 %collective-permute-start.6 = (bf16[128,256]{1,0:T(8,128)(2,1)S(1)}, bf16[128,256]{1,0:T(8,128)(2,1)S(1)}, u32[]{:S(2)}, u32[]{:S(2)}) collective-permute-start(bf16[128,256]{1,0:T(8,128)(2,1)S(1)} %shard_map.111.after.r0), channel_id=1, source_target_pairs={{0,1},{1,2},{2,3},{3,0},{4,5},{5,6},{6,7},{7,4},{8,9},{9,10},{10,1... | collective-permute-start | bytes 196616 | tf_op jit(solution)/shard_map/ppermute | solution.py:337
  50.9 5.5 %collective-permute-start.7 = (bf16[128,256]{1,0:T(8,128)(2,1)S(1)}, bf16[128,256]{1,0:T(8,128)(2,1)S(1)}, u32[]{:S(2)}, u32[]{:S(2)}) collective-permute-start(bf16[128,256]{1,0:T(8,128)(2,1)S(1)} %shard_map.111.after.r0), channel_id=1, source_target_pairs={{0,3},{1,0},{2,1},{3,2},{4,7},{5,4},{6,5},{7,6},{8,11},{9,8},{10,9... | collective-permute-start | bytes 196616 | tf_op jit(solution)/shard_map/ppermute | solution.py:337
  58.5 7.7 %collective-permute-start.13 = (bf16[64,2048]{1,0:T(8,128)(2,1)S(1)}, bf16[64,2048]{1,0:T(8,128)(2,1)S(1)}, u32[]{:S(2)}, u32[]{:S(2)}) collective-permute-start(bf16[64,2048]{1,0:T(8,128)(2,1)S(1)} %get-tuple-element.18), channel_id=1, source_target_pairs={{0,8},{4,28},{8,16},{12,4},{16,24},{20,12},{24,0},{28,20},{1,9},{5... | collective-permute-start | bytes 786440 | tf_op jit(solution)/shard_map/ppermute | solution.py:325
  58.8 9.5 %collective-permute-start.12 = (bf16[64,2048]{1,0:T(8,128)(2,1)S(1)}, bf16[64,2048]{1,0:T(8,128)(2,1)S(1)}, u32[]{:S(2)}, u32[]{:S(2)}) collective-permute-start(bf16[64,2048]{1,0:T(8,128)(2,1)S(1)} %get-tuple-element.16), channel_id=1, source_target_pairs={{0,24},{4,12},{8,0},{12,20},{16,8},{20,28},{24,16},{28,4},{1,25},{... | collective-permute-start | bytes 786440 | tf_op jit(solution)/shard_map/ppermute | solution.py:325
  66.2 7.7 %collective-permute-start.14 = (bf16[64,2048]{1,0:T(8,128)(2,1)S(1)}, bf16[64,2048]{1,0:T(8,128)(2,1)S(1)}, u32[]{:S(2)}, u32[]{:S(2)}) collective-permute-start(bf16[64,2048]{1,0:T(8,128)(2,1)S(1)} %add_convert_fusion.1), channel_id=1, source_target_pairs={{0,8},{4,28},{8,16},{12,4},{16,24},{20,12},{24,0},{28,20},{1,9},{5... | collective-permute-start | bytes 786440 | tf_op jit(solution)/shard_map/ppermute | solution.py:325
